TPU v7x, 32 devices: a whole 2x2x4 slice. The times are simulated.
32 devices in a mesh: nodes: 4 (over x, core), batch: 8 (over z, y).
Axes of the slice: x: 2, y: 2, z: 4, core: 2. Of those that a mesh axis runs over, the one named last changes fastest.
Arguments:
- leaves: float32 [8, 128, 1024], P('nodes', None, 'batch'), may hold values from -340 to 8
- prod_child: int32 [8, 2], replicated, may hold values from 0 to 7
- block_weight: float32 [512, 128, 128], P('nodes'), may hold values from 0.0001 to 0.01
- block_child: int32 [4, 128], P('nodes'), may hold values from 0 to 7
- block_parent: int32 [4, 128], P('nodes'), may hold values from 0 to 3, as said below
- block_count: int32 [4], P('nodes'), may hold values from 32 to 128, as said below
- upper_flow: float32 [16, 128, 1024], P('nodes', None, 'batch'), may hold values from 0.1 to 1
Outputs:
- sum_values: float32 [16, 128, 1024], P('nodes', None, 'batch')
- leaf_flow: float32 [8, 128, 1024], P('nodes', None, 'batch')
- param_flow: float32 [512, 128, 128], P(('nodes', 'batch'))
Inputs may be any that keep to these rules, and one draw needn't show every extreme that they name: `block_parent`: every owner's first 4 slots name its sum groups 0 to 3 in order. `block_count`: some owner has all 128 slots live.
All inputs are finite; a program needn't handle non-finite values.
Results may differ from a plain program's by a relative error of at most 0.0003.
Values sent between devices are 32-bit elements; how exact they have to be, the bound alone decides.
A program may use at most 128 MiB of HBM per device.

v0:
```python
import jax
import jax.numpy as jnp
from jax import lax
from jax.sharding import PartitionSpec as P

very_low = -1e30
high = lax.Precision.HIGHEST


def body(leaves, prod_child, block_weight, block_child, block_parent, block_count, upper_flow):
    group_leaf = leaves.shape[0]
    owners = lax.axis_size("nodes")
    total_leaf = group_leaf * owners
    total_prod = prod_child.shape[0]
    prod_each = total_prod // owners
    sum_each = upper_flow.shape[0]
    blocks = block_weight.shape[0]
    mine = lax.axis_index("nodes")
    first = jax.nn.one_hot(prod_child[:, 0], total_leaf, dtype=jnp.float32)
    second = jax.nn.one_hot(prod_child[:, 1], total_leaf, dtype=jnp.float32)
    select = first + second
    own_select = lax.dynamic_slice_in_dim(select, mine * prod_each, prod_each, 0)
    columns = own_select
    own_prod = jnp.einsum(
        "pg,gjs->pjs",
        columns,
        lax.all_gather(leaves, "nodes", axis=0, tiled=True),
        precision=high,
        preferred_element_type=jnp.float32,
    )
    products = lax.all_gather(own_prod, "nodes", axis=0, tiled=True)
    peak = jnp.max(products, axis=1)
    child = block_child.reshape(-1)
    parent = block_parent.reshape(-1)
    live = jnp.arange(blocks, dtype=jnp.int32) < block_count[0]
    parent_hot = jax.nn.one_hot(parent, sum_each, dtype=jnp.float32) * live[:, None].astype(
        jnp.float32
    )
    child_peak = jnp.where(live[:, None], peak[child], very_low)
    top = jnp.max(jnp.where(parent_hot[:, :, None] > 0.0, child_peak[:, None, :], very_low), axis=0)
    diff = products[child] - top[parent][:, None, :]
    shifted = jnp.exp(jnp.where(live[:, None, None], diff, very_low))
    mixed = jnp.einsum(
        "bij,bjs->bis", block_weight, shifted, precision=high, preferred_element_type=jnp.float32
    )
    total = jnp.einsum(
        "bq,bis->qis", parent_hot, mixed, precision=high, preferred_element_type=jnp.float32
    )
    sum_values = top[:, None, :] + jnp.log(total)
    factor = upper_flow / total
    parent_factor = factor[parent]
    back = jnp.einsum(
        "bij,bis->bjs",
        block_weight,
        parent_factor,
        precision=high,
        preferred_element_type=jnp.float32,
    )
    child_term = shifted * back
    child_hot = jax.nn.one_hot(child, total_prod, dtype=jnp.float32) * live[:, None].astype(
        jnp.float32
    )
    composite = jnp.dot(child_hot, select, precision=high, preferred_element_type=jnp.float32)
    columns = composite
    leaf_flow = lax.psum_scatter(
        jnp.einsum(
            "bg,bjs->gjs", columns, child_term, precision=high, preferred_element_type=jnp.float32
        ),
        "nodes",
        scatter_dimension=0,
        tiled=True,
    )
    param_flow = lax.psum_scatter(
        block_weight
        * jnp.einsum(
            "bis,bjs->bij",
            parent_factor,
            shifted,
            precision=high,
            preferred_element_type=jnp.float32,
        ),
        "batch",
        scatter_dimension=0,
        tiled=True,
    )
    return (sum_values, leaf_flow, param_flow)


def solution(mesh):
    placed = (
        P("nodes", None, "batch"),
        P(),
        P("nodes", None, None),
        P("nodes", None),
        P("nodes", None),
        P("nodes"),
        P("nodes", None, "batch"),
    )
    return jax.shard_map(
        body,
        mesh=mesh,
        in_specs=placed,
        out_specs=(
            P("nodes", None, "batch"),
            P("nodes", None, "batch"),
            P(("nodes", "batch"), None, None),
        ),
        check_vma=False,
    )
```

profile of v0, /device:TPU:0, one launch (start us, length us, event | category | flops | bytes accessed | tf_op | source)
XLA Modules:
  0.0 307.8 jit_solution(12826509481337249558)
XLA Ops:
  7.2 0.8 slice_bitcast_fusion.1
  8.0 8.8 %all_gather.6 = f32[8,128,128]{2,1,0:T(8,128)S(1)} all-gather(f32[2,128,128]{2,1,0:T(8,128)} %param.7), channel_id=1, replica_groups=mesh['nodes'=4,'batch'=8] {'nodes'}, dimensions={0}, use_global_device_ids=true | all-gather | bytes 655360 | tf_op jit(solution)/shard_map/all_gather | solution.py:27
  16.9 0.8 fusion.10
  17.7 7.3 %all_gather.7 = f32[8,128,128]{2,1,0:T(8,128)S(1)} all-gather(f32[2,128,128]{2,1,0:T(8,128)S(1)} %copy.49), channel_id=1, replica_groups=mesh['nodes'=4,'batch'=8] {'nodes'}, dimensions={0}, use_global_device_ids=true | all-gather | bytes 655360 | tf_op jit(solution)/shard_map/all_gather | solution.py:31
  25.0 0.7 fusion.22
  25.7 4.3 %gather_fusion.1 = f32[128,128,128]{2,1,0:T(8,128)} fusion(f32[8,128,128]{2,1,0:T(8,128)S(1)} %all_gather.7, s32[1024]{0:T(1024)S(1)} %pad_clamp_fusion.1), kind=kCustom, calls=%fused_computation.1 | custom fusion | bytes 16777728 | tf_op jit(solution)/shard_map/gather | solution.py:41
  30.0 0.6 gather_fusion
  31.3 9.0 %copy.50 = f32[128,128,128]{1,2,0:T(8,128)} copy(f32[128,128,128]{2,1,0:T(8,128)} %gather_fusion.1) | data formatting | bytes 16777216 | tf_op jit(solution)/shard_map/gather | solution.py:41
  40.3 0.1 broadcast_select_fusion
  40.5 0.1 select_reduce_fusion
  40.6 0.6 gather_fusion.2
  41.2 23.8 %fusion.8 = f32[128,128,128]{1,2,0:T(8,128)} fusion(f32[128,128,128]{2,1,0:T(8,128)} %param.9, f32[128,128,128]{1,2,0:T(8,128)} %copy.50, f32[128,128]{1,0:T(8,128)S(1)} %gather_fusion.2, pred[128]{0:T(512)(128)(4,1)S(1)} %get-tuple-element.22), kind=kOutput, calls=%fused_computation.14 | convolution fusion | flops 3225419776 | bytes 25231488 | tf_op jit(solution)/shard_map/bij,bjs->bis/dot_general | solution.py:43
  65.0 9.4 %copy.51 = f32[128,128,128]{2,0,1:T(8,128)} copy(f32[128,128,128]{1,2,0:T(8,128)} %fusion.8) | data formatting | bytes 16777216 | tf_op jit(solution)/shard_map/bij,bjs->bis/dot_general | solution.py:43
  74.4 6.4 %log_add_fusion = (f32[4,128,128]{2,0,1:T(4,128)S(1)}, f32[4,128,128]{2,0,1:T(4,128)S(1)}) fusion(f32[4,128]{1,0:T(4,128)S(1)} %select_reduce_fusion, f32[128,128,128]{2,0,1:T(8,128)} %copy.51, f32[128]{0:T(128)S(1)} %get-tuple-element.23, s32[128]{0:T(128)S(1)} %bitcast.38), kind=kOutput, calls=%fused_computation.20 | convolution fusion | flops 100729856 | bytes 8915968 | tf_op jit(solution)/shard_map/bq,bis->qis/dot_general | solution.py:46
  80.9 4.3 %gather_fusion.3 = f32[128,128,128]{2,1,0:T(8,128)} fusion(f32[4,128,128]{2,1,0:T(8,128)S(1)} %copy_divide_fusion, s32[1024]{0:T(1024)S(1)} %pad_clamp_fusion), kind=kCustom, calls=%fused_computation.3 | custom fusion | bytes 16777728 | tf_op jit(solution)/shard_map/gather | solution.py:51
  85.2 22.4 %bitcast_multiply_fusion = f32[128,128,128]{1,2,0:T(8,128)} fusion(f32[128,128,128]{1,2,0:T(8,128)} %copy.50, f32[128,128]{1,0:T(8,128)S(1)} %gather_fusion.2, pred[128]{0:T(512)(128)(4,1)S(1)} %get-tuple-element.22, f32[128,128,128]{2,1,0:T(8,128)} %gather_fusion.3, f32[128,128,128]{2,1,0:T(8,128)} %param.9), kind=kOutput, calls=%fused_computation.4 | convolution fusion | flops 3227516928 | bytes 33620096 | tf_op jit(solution)/shard_map/bij,bis->bjs/dot_general | solution.py:52
  107.5 9.4 %copy.54 = f32[128,128,128]{2,0,1:T(8,128)} copy(f32[128,128,128]{1,2,0:T(8,128)} %bitcast_multiply_fusion) | data formatting | bytes 16777216 | tf_op jit(solution)/shard_map/mul | solution.py:59
  116.9 0.3 convolution_bitcast_fusion
  117.2 6.4 %fusion.30 = f32[8,128,128]{2,0,1:T(8,128)S(1)} fusion(f32[128,8,1]{0,1,2:T(8,128)S(1)} %convolution_bitcast_fusion, f32[128,128,128]{2,0,1:T(8,128)} %copy.54), kind=kOutput, calls=%fused_computation.55 | convolution fusion | flops 201326592 | bytes 8916992 | tf_op jit(solution)/shard_map/bg,bjs->gjs/dot_general | solution.py:66
  123.5 0.9 copy.55
  124.6 17.2 %fusion.9 = f32[128,128,128]{2,1,0:T(8,128)} fusion(f32[128,128,128]{2,1,0:T(8,128)} %param.9, f32[128,128,128]{2,1,0:T(8,128)} %gather_fusion.3, f32[128,128,128]{1,2,0:T(8,128)} %copy.50, f32[128,128]{1,0:T(8,128)S(1)} %gather_fusion.2, pred[128]{0:T(512)(128)(4,1)S(1)} %get-tuple-element.22), kind=kOutput, calls=%fused_computation.15 | convolution fusion | flops 3227516928 | bytes 33620096 | tf_op jit(solution)/shard_map/bis,bjs->bij/dot_general | solution.py:75
  141.8 0.7 copy.57
  142.5 4.7 %reduce-scatter.3.cloned.1.call-done = f32[2,128,128]{2,1,0:T(8,128)} async-done(((f32[8,128,128]{2,1,0:T(8,128)}), f32[2,128,128]{2,1,0:T(8,128)}) %reduce-scatter.3.cloned.1.call-update) | async-done | bytes 131088 | tf_op jit(solution)/shard_map/reduce_scatter | solution.py:65
  147.2 153.8 %reduce-scatter.5.cloned.1.call-done = f32[16,128,128]{2,1,0:T(8,128)} async-done(((f32[128,128,128]{2,1,0:T(8,128)}), f32[16,128,128]{2,1,0:T(8,128)}) %reduce-scatter.5.cloned.1.call-update) | async-done | bytes 1048592 | tf_op jit(solution)/shard_map/reduce_scatter | solution.py:73
  (19 shorter events, 0.3 us)
Async XLA Ops:
  7.2 140.0 %reduce-scatter.3.cloned.1.call-start = ((), (), s32[]{:S(2)}) async-start(), calls=%async_computation.2 | async-start | bytes 655360 | tf_op jit(solution)/shard_map/reduce_scatter | solution.py:65
  25.7 5.6 %copy-start.1 = (s32[1,128]{1,0:T(1,128)S(1)}, s32[1,128]{1,0:T(1,128)}, u32[]{:S(2)}) copy-start(s32[1,128]{1,0:T(1,128)} %param.11) | copy-start | bytes 1540
  74.4 6.4 %copy-start = (f32[4,128,128]{2,1,0:T(8,128)S(1)}, f32[4,128,128]{2,1,0:T(8,128)}, u32[]{:S(2)}) copy-start(f32[4,128,128]{2,1,0:T(8,128)} %param.13) | copy-start | bytes 786436
  107.5 9.4 %copy-start.2 = (s32[1,128]{1,0:T(1,128)S(1)}, s32[1,128]{1,0:T(1,128)}, u32[]{:S(2)}) copy-start(s32[1,128]{1,0:T(1,128)} %param.10) | copy-start | bytes 1540
  124.5 176.4 %reduce-scatter.5.cloned.1.call-start = ((), (), s32[]{:S(2)}) async-start(), calls=%async_computation.3 | async-start | bytes 9437184 | tf_op jit(solution)/shard_map/reduce_scatter | solution.py:73
Sparse Core Ops, SparseCore 0:
  124.6 22.4 reduce-scatter.2
  151.8 149.0 reduce-scatter.4
where the time goes:
time: 308 us
  waiting for transfers between devices  158 us (51%)
  matrix products  77.1 us (25%)
  local copies, waits for them, and re-layouts  40.1 us (13%)
  blocking collectives  16.1 us (5%)
  between operations  14.8 us (5%)
    reduce_scatter x1, waiting for transfers between devices, body(): lax.psum_scatter(block_weight * jnp.einsum('bis,bjs->bij', parent_factor,...  154 us
    dot_general x1, matrix products, body(): jnp.einsum('bij,bjs->bis', block_weight, shifted, precision=high, preferr...  23.8 us
    dot_general x1, matrix products, body(): jnp.einsum('bij,bis->bjs', block_weight, parent_factor, precision=high, p...  22.4 us
    dot_general x1, matrix products, body(): jnp.einsum('bis,bjs->bij', parent_factor, shifted, precision=high, prefer...  17.2 us
    gather x3, local copies, waits for them, and re-layouts, body(): diff = products[child] - top[parent][:, None, :]  13.9 us
    dot_general x1, local copies, waits for them, and re-layouts, body(): jnp.einsum('bij,bjs->bis', block_weight, shifted, precision=high, preferr...  9.37 us
    mul x1, local copies, waits for them, and re-layouts, body(): child_term = shifted * back  9.37 us
    all_gather x1, blocking collectives, body(): lax.all_gather(leaves, 'nodes', axis=0, tiled=True)  8.82 us
  transfers between devices with their start and end apart: 2, of which 2 were waited for; matrix products, arithmetic and copies ran while one was open for 6% of the time, Pallas kernels for 0%

commit v1 on v0

v1 whole, which is shorter than its diff:
```python
import jax
import jax.numpy as jnp
from jax import lax
from jax.sharding import PartitionSpec as P

very_low = -1e30
high = lax.Precision.HIGH


def body(leaves, prod_child, block_weight, block_child, block_parent, block_count, upper_flow):
    total_prod = prod_child.shape[0]
    sum_each = upper_flow.shape[0]
    blocks = block_weight.shape[0]
    keep = blocks // lax.axis_size("batch")
    every = lax.all_gather(leaves, "nodes", axis=0, tiled=True)
    select = jax.nn.one_hot(prod_child[:, 0], every.shape[0], dtype=jnp.float32) + jax.nn.one_hot(
        prod_child[:, 1], every.shape[0], dtype=jnp.float32
    )
    products = every[prod_child[:, 0]] + every[prod_child[:, 1]]
    peak = jnp.max(products, axis=1)
    child = block_child.reshape(-1)
    parent = block_parent.reshape(-1)
    live = jnp.arange(blocks, dtype=jnp.int32) < block_count[0]
    pair = parent * total_prod + child
    pairs = sum_each * total_prod
    hot = jnp.where(live[:, None], jax.nn.one_hot(pair, pairs, dtype=jnp.float32), 0.0)
    weight = jnp.einsum(
        "bp,bij->pij", hot, block_weight, precision=high, preferred_element_type=jnp.float32
    ).reshape(sum_each, total_prod, *block_weight.shape[1:])
    has = (jnp.max(hot, axis=0) > 0.0).reshape(sum_each, total_prod)[:, :, None]
    top = jnp.max(jnp.where(has, peak[None], very_low), axis=1)
    scale = jnp.where(has, jnp.exp(jnp.where(has, peak[None] - top[:, None], 0.0)), 0.0)
    unit = jnp.exp(products - peak[:, None])
    total = jnp.einsum(
        "qcij,qcjs->qis",
        weight,
        unit[None] * scale[:, :, None],
        precision=high,
        preferred_element_type=jnp.float32,
    )
    sum_values = top[:, None, :] + jnp.log(total)
    factor = upper_flow / total
    scaled = factor[:, None] * scale[:, :, None]
    outer = jnp.einsum(
        "qcis,cjs->qcij", scaled, unit, precision=high, preferred_element_type=jnp.float32
    )
    outer = lax.psum(outer.reshape(pairs, *block_weight.shape[1:]), "batch")
    back = jnp.einsum(
        "qcij,qcis->cjs", weight, scaled, precision=high, preferred_element_type=jnp.float32
    )
    leaf_flow = lax.psum_scatter(
        jnp.einsum(
            "cg,cjs->gjs",
            select,
            unit * back,
            precision=lax.Precision.HIGHEST,
            preferred_element_type=jnp.float32,
        ),
        "nodes",
        scatter_dimension=0,
        tiled=True,
    )
    first = lax.axis_index("batch") * keep
    own = lax.dynamic_slice_in_dim(block_weight, first, keep, 0)
    own_pair = lax.dynamic_slice_in_dim(pair, first, keep, 0)
    own_live = lax.dynamic_slice_in_dim(live, first, keep, 0)
    param_flow = jnp.where(own_live[:, None, None], own * outer[own_pair], 0.0)
    return (sum_values, leaf_flow, param_flow)


def solution(mesh):
    placed = (
        P("nodes", None, "batch"),
        P(),
        P("nodes", None, None),
        P("nodes", None),
        P("nodes", None),
        P("nodes"),
        P("nodes", None, "batch"),
    )
    return jax.shard_map(
        body,
        mesh=mesh,
        in_specs=placed,
        out_specs=(
            P("nodes", None, "batch"),
            P("nodes", None, "batch"),
            P(("nodes", "batch"), None, None),
        ),
        check_vma=False,
    )
```

time: 308 us -> 154 us (0.50)
  waiting for transfers between devices: 158 us -> 98 us
  matrix products: 77.1 us -> 19.1 us
  local copies, waits for them, and re-layouts: 40.1 us -> 8.08 us
  blocking collectives: 16.1 us -> 8.83 us
    reduce_scatter x2 -> x1, waiting for transfers between devices: 158 us -> 0.01 us  [body(): lax.psum_scatter(jnp.einsum('cg,cjs->gjs', select, unit * back, precision...]
    psum x0 -> x1, waiting for transfers between devices: none -> 98 us  [body(): outer = lax.psum(outer.reshape(pairs, *block_weight.shape[1:]), 'batch')]
    dot_general x7 -> x5, matrix products: 77.1 us -> 19.1 us  [the longest x1 10.3 us: body(): jnp.einsum('bp,bij->pij', hot, block_weight, precision=high, preferred_el...]
    gather x5 -> x3, local copies, waits for them, and re-layouts: 18.9 us -> 3.37 us  [the longest x1 2.2 us: body(): param_flow = jnp.where(own_live[:, None, None], own * outer[own_pair], 0.0)]
    dot_general x3 -> x1, local copies, waits for them, and re-layouts: 10.3 us -> 0.89 us  [body(): jnp.einsum('cg,cjs->gjs', select, unit * back, precision=lax.Precision.HI...]
    mul x1 -> x0, local copies, waits for them, and re-layouts: 9.37 us -> none  [body(): child_term = shifted * back]
    all_gather x2 -> x1, blocking collectives: 16.1 us -> 8.83 us  [body(): every = lax.all_gather(leaves, 'nodes', axis=0, tiled=True)]
  transfers between devices with their start and end apart: 2 -> 2, of which waited for: 2 -> 1; matrix products, arithmetic and copies ran while one was open for 6% -> 6% of each run, Pallas kernels for 0% -> 0%
where the time goes in v1:
time: 154 us
  waiting for transfers between devices  98 us (64%)
  matrix products  19.1 us (12%)
  between operations  16.3 us (11%)
  blocking collectives  8.83 us (6%)
  local copies, waits for them, and re-layouts  8.08 us (5%)
  other arithmetic  3.64 us (2%)
    psum x1, waiting for transfers between devices, body(): outer = lax.psum(outer.reshape(pairs, *block_weight.shape[1:]), 'batch')  98 us
    dot_general x1, matrix products, body(): jnp.einsum('bp,bij->pij', hot, block_weight, precision=high, preferred_el...  10.3 us
    all_gather x1, blocking collectives, body(): every = lax.all_gather(leaves, 'nodes', axis=0, tiled=True)  8.83 us
  transfers between devices with their start and end apart: 2, of which 1 were waited for; matrix products, arithmetic and copies ran while one was open for 6% of the time, Pallas kernels for 0%

profile of v1, /device:TPU:0, one launch (start us, length us, event | category | flops | bytes accessed | tf_op | source)
XLA Modules:
  0.0 154.2 jit_solution(17261397237577175239)
XLA Ops:
  8.1 8.8 %all_gather.3 = f32[8,128,128]{2,1,0:T(8,128)S(1)} all-gather(f32[2,128,128]{2,1,0:T(8,128)} %param.7), channel_id=1, replica_groups=mesh['nodes'=4,'batch'=8] {'nodes'}, dimensions={0}, use_global_device_ids=true | all-gather | bytes 655360 | tf_op jit(solution)/shard_map/all_gather | solution.py:15
  16.9 0.8 slice_bitcast_fusion.1
  17.7 0.6 gather_fusion
  18.3 0.6 gather_fusion.1
  19.5 0.1 fusion.39
  19.7 0.1 gt.15
  19.7 0.1 copy.23
  19.8 10.3 %fusion.13 = f32[4,8,128,128]{3,1,0,2:T(8,128)S(1)} fusion(f32[128,128,128]{2,1,0:T(8,128)} %param.9, s32[128]{0:T(128)S(1)} %bitcast.39, pred[128]{0:T(512)(128)(4,1)S(1)} %iota_compare_fusion.6), kind=kOutput, calls=%fused_computation.14 | convolution fusion | flops 402665472 | bytes 10486400 | tf_op jit(solution)/shard_map/bp,bij->pij/dot_general | solution.py:27
  30.2 0.1 select_reduce_fusion
  30.3 0.1 exponential_select_fusion
  30.4 0.1 subtract_exponential_fusion
  30.5 0.6 copy-done
  31.1 2.9 %fusion.53 = (f32[4,128,128]{2,1,0:T(8,128)S(1)}, f32[4,128,128]{2,1,0:T(8,128)}) fusion(f32[4,128,128]{2,1,0:T(8,128)S(1)} %copy-done, f32[4,128]{1,0:T(4,128)S(1)} %select_reduce_fusion, f32[4,8,128,128]{3,1,0,2:T(8,128)S(1)} %fusion.13, f32[4,8,128]{2,0,1:T(4,128)S(1)} %exponential_select_fusion, f32[8,128,128]{2,1,0:T(8,128)S(1)} %subtract_exponential_fusion), kind=kOutput, calls=%fused_computation.61 | convolution fusion | flops 403308544 | bytes 3426304 | tf_op jit(solution)/shard_map/qcij,qcjs->qis/dot_general | solution.py:34
  34.0 2.3 %fusion.10 = f32[4,8,128,128]{2,3,0,1:T(8,128)} fusion(f32[4,128,128]{2,1,0:T(8,128)S(1)} %get-tuple-element.11, f32[4,8,128]{2,0,1:T(4,128)S(1)} %exponential_select_fusion, f32[8,128,128]{2,1,0:T(8,128)S(1)} %subtract_exponential_fusion), kind=kOutput, calls=%fused_computation.13 | convolution fusion | flops 403177472 | bytes 2899968 | tf_op jit(solution)/shard_map/qcis,cjs->qcij/dot_general | solution.py:44
  36.3 2.9 %copy.30 = f32[4,8,128,128]{3,2,1,0:T(8,128)} copy(f32[4,8,128,128]{2,3,0,1:T(8,128)} %fusion.10) | data formatting | bytes 4194304 | tf_op jit(solution)/shard_map/qcis,cjs->qcij/transpose | solution.py:44
  39.3 0.2 reduce-scatter.2.cloned.1.call-start
  39.5 2.8 %fusion.21 = f32[8,128,128]{2,1,0:T(8,128)S(1)} fusion(f32[8,128,128]{2,1,0:T(8,128)S(1)} %subtract_exponential_fusion, f32[4,8,128,128]{3,1,0,2:T(8,128)S(1)} %fusion.13, f32[4,128,128]{2,1,0:T(8,128)S(1)} %get-tuple-element.11, f32[4,8,128]{2,0,1:T(4,128)S(1)} %exponential_select_fusion), kind=kOutput, calls=%fused_computation.16 | convolution fusion | flops 403308544 | bytes 3424256 | tf_op jit(solution)/shard_map/qcij,qcis->cjs/dot_general | solution.py:48
  42.3 0.8 fusion.36
  43.1 0.9 copy.29
  44.0 0.1 dynamic_slice.11
  44.1 0.1 compare_select_fusion
  44.2 98.0 %all-reduce.2.cloned.1.call-done = f32[32,128,128]{2,1,0:T(8,128)} async-done(((f32[32,128,128]{2,1,0:T(8,128)}), f32[32,128,128]{2,1,0:T(8,128)}) %all-reduce.2.cloned.1.call-update) | async-done | bytes 2097168 | tf_op jit(solution)/shard_map/psum | solution.py:47
  142.2 2.2 %gather_fusion.2 = f32[16,128,128]{2,1,0:T(8,128)S(1)} fusion(f32[32,128,128]{2,1,0:T(8,128)} %all-reduce.2.cloned.1.call-done, s32[1024]{0:T(1024)S(1)} %pad_clamp_fusion), kind=kCustom, calls=%fused_computation.2 | custom fusion | bytes 2097216 | tf_op jit(solution)/shard_map/gather | solution.py:67
  144.4 2.3 %multiply_select_fusion = f32[16,128,128]{2,1,0:T(8,128)} fusion(f32[16,128,128]{2,1,0:T(8,128)S(1)} %gather_fusion.2, f32[128,128,128]{2,1,0:T(8,128)} %param.9, s32[]{:T(128)S(6)} %select_n.49, pred[16]{0:T(512)(128)(4,1)S(1)} %dynamic_slice.11), kind=kLoop, calls=%fused_computation.18 | loop fusion | flops 524288 | bytes 3145748 | tf_op jit(solution)/shard_map/jit(_where)/select_n | solution.py:67
  (15 shorter events, 0.2 us)
Async XLA Ops:
  8.0 11.5 %copy-start.1 = (s32[1,128]{1,0:T(1,128)S(1)}, s32[1,128]{1,0:T(1,128)}, u32[]{:S(2)}) copy-start(s32[1,128]{1,0:T(1,128)} %param.10) | copy-start | bytes 1540
  8.0 11.5 %copy-start.2 = (s32[1,128]{1,0:T(1,128)S(1)}, s32[1,128]{1,0:T(1,128)}, u32[]{:S(2)}) copy-start(s32[1,128]{1,0:T(1,128)} %param.11) | copy-start | bytes 1540
  8.0 134.1 %all-reduce.2.cloned.1.call-start = ((), (), s32[]{:S(2)}) async-start(), calls=%async_computation.2 | async-start | bytes 4194304 | tf_op jit(solution)/shard_map/psum | solution.py:47
  30.2 1.0 copy-start
  39.3 107.4 %reduce-scatter.2.cloned.1.call-start = ((), (), s32[]{:S(2)}) async-start(), calls=%async_computation.1 | async-start | bytes 655360 | tf_op jit(solution)/shard_map/reduce_scatter | solution.py:51
Sparse Core Ops, SparseCore 0:
  39.4 102.7 all-reduce.1
Sparse Core Ops, SparseCore 1:
  44.1 22.5 reduce-scatter.1

commit v2 on v1

--- a/solution.py
+++ b/solution.py
@@ -1,6 +1,8 @@
 import jax
 import jax.numpy as jnp
 from jax import lax
+from jax.experimental import pallas as pl
+from jax.experimental.pallas import tpu as pltpu
 from jax.sharding import PartitionSpec as P
 
 very_low = -1e30
@@ -68,6 +70,376 @@
     return (sum_values, leaf_flow, param_flow)
 
 
+MESH = pl.DeviceIdType.MESH
+f32, bf16 = jnp.float32, jnp.bfloat16
+
+
+def split(value):
+    top_part = value.astype(bf16)
+    return top_part, (value - top_part.astype(f32)).astype(bf16)
+
+
+def dot3(a, b, dims):
+    (a_hi, a_lo), (b_hi, b_lo) = a, b
+    dot = lambda p, q: lax.dot_general(p, q, (dims, ((), ())), preferred_element_type=f32)
+    return dot(a_hi, b_hi) + dot(a_hi, b_lo) + dot(a_lo, b_hi)
+
+
+def weight_kernel(pair_ref, count_ref, w_ref, hi_ref, lo_ref, acc):
+    step = pl.program_id(0)
+    size = w_ref.shape[0]
+
+    @pl.when(step == 0)
+    def _():
+        acc[...] = jnp.zeros_like(acc)
+
+    def add(b, carry):
+        at = pair_ref[step * size + b]
+        acc[at] = acc[at] + w_ref[b]
+        return carry
+
+    lax.fori_loop(0, jnp.clip(count_ref[0] - step * size, 0, size), add, 0)
+
+    @pl.when(step == pl.num_programs(0) - 1)
+    def _():
+        def out(p, carry):
+            hi_ref[p], lo_ref[p] = split(acc[p])
+            return carry
+
+        lax.fori_loop(0, acc.shape[0], out, 0)
+
+
+def sum_weights(block_weight, pair, count, pairs):
+    blocks, rows, columns = block_weight.shape
+    size = 16
+    whole = pl.BlockSpec((pairs, rows, columns), lambda i, *_: (0, 0, 0))
+    return pl.pallas_call(
+        weight_kernel,
+        grid_spec=pltpu.PrefetchScalarGridSpec(
+            num_scalar_prefetch=2,
+            grid=(blocks // size,),
+            in_specs=[pl.BlockSpec((size, rows, columns), lambda i, *_: (i, 0, 0))],
+            out_specs=[whole, whole],
+            scratch_shapes=[pltpu.VMEM((pairs, rows, columns), f32)],
+        ),
+        out_shape=[jax.ShapeDtypeStruct((pairs, rows, columns), bf16)] * 2,
+        compiler_params=pltpu.CompilerParams(vmem_limit_bytes=24 << 20),
+    )(pair, count, block_weight)
+
+
+def main_kernel(
+    child_of, pair_of, alive, select, leaves, w_hi, w_lo, mask, upper, own_weight,
+    sum_values, leaf_flow, param_flow,
+    L, F, cur, fcur, u_hi, u_lo, peaks, scale, total, outer, part, got_core, mid, got_x,
+    recv_l, send_lx, send_lc, send_ly, send_lz, recv_f, send_fy, send_fz, send_core, recv_core, send_x, recv_x,
+):
+    n, t = lax.axis_index("nodes"), lax.axis_index("batch")
+    x, k, z, y = n // 2, n % 2, t // 2, t % 2
+    depth = 4
+    nx, nc, nxc = (1 - x) * 2 + k, x * 2 + 1 - k, (1 - x) * 2 + 1 - k
+    by_x, by_core, by_y = (nx, t), (nc, t), (n, z * 2 + 1 - y)
+    by_z = ((n, t - 2), (n, t + 2))
+    has_z = (z > 0, z < depth - 1)
+    prods, sums = u_hi.shape[0], upper.shape[0]
+    wide = upper.shape[1]
+    keep = outer.shape[0]
+    very = f32(very_low)
+
+    L[t * 4 + n] = leaves[...]
+    barrier = pltpu.get_barrier_semaphore()
+    for partner in (by_x, by_core, by_y):
+        pl.semaphore_signal(barrier, inc=1, device_id=partner, device_id_type=MESH)
+    for side in range(2):
+        @pl.when(has_z[side])
+        def _():
+            pl.semaphore_signal(barrier, inc=1, device_id=by_z[side], device_id_type=MESH)
+    pl.semaphore_wait(barrier, 3 + (z > 0).astype(jnp.int32) + (z < depth - 1).astype(jnp.int32))
+
+    def remote(src, dst, send, recv, to):
+        return pltpu.make_async_remote_copy(
+            src_ref=src, dst_ref=dst, send_sem=send, recv_sem=recv, device_id=to, device_id_type=MESH
+        )
+
+    def leaf_to(nn, tt, send, to):
+        at = L.at[tt * 4 + nn]
+        return remote(at, at, send, recv_l.at[tt * 4 + nn], to)
+
+    def leaf_x(tt):
+        return leaf_to(n, tt, send_lx.at[tt], by_x)
+
+    def leaf_c(nn, which, tt):
+        return leaf_to(nn, tt, send_lc.at[which * 8 + tt], by_core)
+
+    def leaf_y(zz):
+        return leaf_to(n, zz * 2 + y, send_ly.at[zz], by_y)
+
+    def leaf_z(zz, side):
+        return leaf_to(n, zz * 2 + y, send_lz.at[side * depth + zz], by_z[side])
+
+    def flow_to(tt, send, to):
+        at = F.at[tt]
+        return remote(at, at, send, recv_f.at[tt], to)
+
+    def flow_y(zz):
+        return flow_to(zz * 2 + y, send_fy.at[zz], by_y)
+
+    def flow_z(zz, side):
+        return flow_to(zz * 2 + y, send_fz.at[side * depth + zz], by_z[side])
+
+    def arrived_l(nn, tt):
+        leaf_to(nn, tt, send_lx.at[tt], by_x).wait_recv()
+
+    def arrived_f(tt):
+        flow_to(tt, send_fy.at[0], by_y).wait_recv()
+
+    def spread(tt):
+        leaf_x(tt).start()
+        leaf_c(n, 0, tt).start()
+
+    def gather(tt):
+        arrived_l(nx, tt)
+        leaf_c(nx, 1, tt).start()
+        arrived_l(nc, tt)
+        arrived_l(nxc, tt)
+
+    def units(tt):
+        cur[...] = L[pl.ds(tt * 4, 4)].reshape(cur.shape)
+
+        def one(c, carry):
+            prod = cur[child_of[2 * c]] + cur[child_of[2 * c + 1]]
+            peak = jnp.max(prod, axis=0, keepdims=True)
+            peaks[c] = peak
+            u_hi[c], u_lo[c] = split(jnp.exp(prod - peak))
+            return carry
+
+        lax.fori_loop(0, prods, one, 0)
+        tops = []
+        for q in range(sums):
+            on = mask[q] > 0.0
+            top = jnp.max(jnp.where(on, peaks[...], very), axis=0, keepdims=True)
+            scale[q] = jnp.where(on, jnp.exp(jnp.where(on, peaks[...] - top, 0.0)), 0.0)
+            tops.append(top[0])
+        return tops
+
+    def outers(tt, first):
+        fcur[...] = F[tt]
+
+        def one(b, carry):
+            q, c = pair_of[2 * (t * keep + b)], pair_of[2 * (t * keep + b) + 1]
+            f = split(fcur[q] * scale[q, c])
+            value = dot3(f, (u_hi[c], u_lo[c]), ((1,), (1,)))
+            outer[b] = value if first else outer[b] + value
+            return carry
+
+        lax.fori_loop(0, keep, one, 0)
+
+    leaf_x(t).start()
+    leaf_c(n, 0, t).start()
+    for side in range(2):
+        @pl.when(has_z[side])
+        def _():
+            leaf_z(z, side).start()
+    leaf_y(z).start()
+    gather(t)
+    tops = units(t)
+    total[...] = jnp.zeros_like(total)
+
+    def ahead(c, carry):
+        value = dot3((w_hi[c], w_lo[c]), (u_hi[c], u_lo[c]), ((1,), (0,)))
+        for q in range(sums):
+            rows = pl.ds(q * wide, wide)
+            total[rows] += value[q * wide : (q + 1) * wide] * scale[q, c]
+        return carry
+
+    lax.fori_loop(0, prods, ahead, 0)
+    for q in range(sums):
+        tot = total[pl.ds(q * wide, wide)]
+        sum_values[q] = tops[q] + jnp.log(tot)
+        F[t, q] = upper[q] / tot
+    for side in range(2):
+        @pl.when(has_z[side])
+        def _():
+            flow_z(z, side).start()
+    flow_y(z).start()
+
+    part[...] = jnp.zeros_like(part)
+
+    def behind(c, carry):
+        f = jnp.concatenate([F[t, q] * scale[q, c] for q in range(sums)], axis=0)
+        value = dot3((w_hi[c], w_lo[c]), split(f), ((0,), (0,)))
+        value = value * (u_hi[c].astype(f32) + u_lo[c].astype(f32))
+        for g in range(part.shape[0]):
+            part[g] += value * select[c * part.shape[0] + g]
+        return carry
+
+    lax.fori_loop(0, prods, behind, 0)
+
+    def core_copy(xx):
+        return remote(
+            part.at[pl.ds(2 * (xx * 2 + 1 - k), 2)], got_core.at[xx], send_core.at[xx], recv_core.at[xx], by_core
+        )
+
+    for xx in range(2):
+        core_copy(xx).start()
+
+    outers(t, True)
+    for xx in range(2):
+        core_copy(xx).wait_recv()
+        mid[xx] = part[pl.ds(2 * (xx * 2 + k), 2)] + got_core[xx]
+    x_copy = remote(mid.at[1 - x], got_x, send_x, recv_x, by_x)
+    x_copy.start()
+
+    def other(zz):
+        tt = zz * 2 + 1 - y
+        arrived_l(n, tt)
+        spread(tt)
+        gather(tt)
+        arrived_f(tt)
+        units(tt)
+        outers(tt, False)
+
+    other(z)
+
+    def hop(step, carry):
+        places = (z - step, z + step)
+        exists = (z - step >= 0, z + step < depth)
+        for side in range(2):
+            zz = places[side]
+            @pl.when(exists[side])
+            def _():
+                tt = zz * 2 + y
+                arrived_l(n, tt)
+                spread(tt)
+                leaf_y(zz).start()
+                @pl.when(has_z[1 - side])
+                def _():
+                    leaf_z(zz, 1 - side).start()
+                arrived_f(tt)
+                flow_y(zz).start()
+                @pl.when(has_z[1 - side])
+                def _():
+                    flow_z(zz, 1 - side).start()
+        for side in range(2):
+            zz = places[side]
+            @pl.when(exists[side])
+            def _():
+                tt = zz * 2 + y
+                gather(tt)
+                units(tt)
+                outers(tt, False)
+                other(zz)
+        return carry
+
+    lax.fori_loop(1, depth, hop, 0)
+
+    x_copy.wait_recv()
+    leaf_flow[...] = mid[x] + got_x[...]
+
+    def finish(b, carry):
+        param_flow[b] = own_weight[b] * outer[b] * alive[t * keep + b]
+        return carry
+
+    lax.fori_loop(0, keep, finish, 0)
+
+    for xx in range(2):
+        core_copy(xx).wait_send()
+    x_copy.wait_send()
+
+    def sent(tt, carry):
+        leaf_x(tt).wait_send()
+        leaf_c(n, 0, tt).wait_send()
+        leaf_c(nx, 1, tt).wait_send()
+        return carry
+
+    lax.fori_loop(0, 2 * depth, sent, 0)
+
+    def sent_z(zz, carry):
+        leaf_y(zz).wait_send()
+        flow_y(zz).wait_send()
+        @pl.when((zz >= z) & has_z[0])
+        def _():
+            leaf_z(zz, 0).wait_send()
+            flow_z(zz, 0).wait_send()
+        @pl.when((zz <= z) & has_z[1])
+        def _():
+            leaf_z(zz, 1).wait_send()
+            flow_z(zz, 1).wait_send()
+        return carry
+
+    lax.fori_loop(0, depth, sent_z, 0)
+
+
+def fused(leaves, prod_child, block_weight, block_child, block_parent, block_count, upper_flow):
+    group, wide, samples = leaves.shape
+    prods, sums = prod_child.shape[0], upper_flow.shape[0]
+    blocks = block_weight.shape[0]
+    owners, batches = lax.axis_size("nodes"), lax.axis_size("batch")
+    keep = blocks // batches
+    child, parent = block_child.reshape(-1), block_parent.reshape(-1)
+    live = jnp.arange(blocks, dtype=jnp.int32) < block_count[0]
+    w_hi, w_lo = sum_weights(block_weight, child * sums + parent, block_count, prods * sums)
+    w_hi = w_hi.reshape(prods, sums * wide, wide)
+    w_lo = w_lo.reshape(prods, sums * wide, wide)
+    hit = live[:, None] & (
+        (parent * prods + child)[:, None] == jnp.arange(sums * prods, dtype=jnp.int32)[None]
+    )
+    mask = jnp.max(hit.astype(f32), axis=0).reshape(sums, prods, 1, 1)
+    mask = jnp.broadcast_to(mask, (sums, prods, 1, samples))
+    select = (
+        jax.nn.one_hot(prod_child[:, 0], owners * group, dtype=f32)
+        + jax.nn.one_hot(prod_child[:, 1], owners * group, dtype=f32)
+    ).reshape(-1)
+    own = lax.dynamic_slice_in_dim(block_weight, lax.axis_index("batch") * keep, keep, 0)
+    pair_of = jnp.stack([parent, child], axis=1).reshape(-1)
+    smem, vmem = pl.BlockSpec(memory_space=pltpu.SMEM), pl.BlockSpec(memory_space=pltpu.VMEM)
+    dma = lambda *dims: pltpu.SemaphoreType.DMA(dims)
+    tile = (wide, samples)
+    return pl.pallas_call(
+        main_kernel,
+        in_specs=[smem] * 4 + [vmem] * 6,
+        out_specs=[vmem] * 3,
+        out_shape=[
+            jax.ShapeDtypeStruct(upper_flow.shape, f32),
+            jax.ShapeDtypeStruct(leaves.shape, f32),
+            jax.ShapeDtypeStruct(own.shape, f32),
+        ],
+        scratch_shapes=[
+            pltpu.VMEM((batches * owners, group, *tile), f32),
+            pltpu.VMEM((batches, sums, *tile), f32),
+            pltpu.VMEM((owners * group, *tile), f32),
+            pltpu.VMEM((sums, *tile), f32),
+            pltpu.VMEM((prods, *tile), bf16),
+            pltpu.VMEM((prods, *tile), bf16),
+            pltpu.VMEM((prods, 1, samples), f32),
+            pltpu.VMEM((sums, prods, 1, samples), f32),
+            pltpu.VMEM((sums * wide, samples), f32),
+            pltpu.VMEM(own.shape, f32),
+            pltpu.VMEM((owners * group, *tile), f32),
+            pltpu.VMEM((2, group, *tile), f32),
+            pltpu.VMEM((2, group, *tile), f32),
+            pltpu.VMEM((group, *tile), f32),
+            dma(batches * owners),
+            dma(batches),
+            dma(2 * batches),
+            dma(batches // 2),
+            dma(batches),
+            dma(batches),
+            dma(batches // 2),
+            dma(batches),
+            dma(2),
+            dma(2),
+            pltpu.SemaphoreType.DMA,
+            pltpu.SemaphoreType.DMA,
+        ],
+        compiler_params=pltpu.CompilerParams(
+            collective_id=0, has_side_effects=True, vmem_limit_bytes=32 << 20
+        ),
+    )(
+        prod_child.reshape(-1), pair_of, live.astype(f32), select,
+        leaves, w_hi, w_lo, mask, upper_flow, own,
+    )
+
+
 def solution(mesh):
     placed = (
         P("nodes", None, "batch"),
@@ -78,8 +450,9 @@
         P("nodes"),
         P("nodes", None, "batch"),
     )
+    small = dict(mesh.shape) == {"nodes": 4, "batch": 8}
     return jax.shard_map(
-        body,
+        fused if small else body,
         mesh=mesh,
         in_specs=placed,
         out_specs=(

time: 154 us -> 103 us (0.67)
  waiting for transfers between devices: 98 us -> 0 us
  Pallas kernels: 0 us -> 90.9 us
  matrix products: 19.1 us -> 0 us
  between operations: 16.3 us -> 1.41 us
  blocking collectives: 8.83 us -> 0 us
  other arithmetic: 3.64 us -> 1.55 us
    psum x1 -> x0, waiting for transfers between devices: 98 us -> none  [body(): outer = lax.psum(outer.reshape(pairs, *block_weight.shape[1:]), 'batch')]
    pallas_call x0 -> x2, Pallas kernels: none -> 90.9 us  [the longest x1 88.3 us: fused(): pl.pallas_call(main_kernel, in_specs=[smem] * 4 + [vmem] * 6, out_specs=[...]
    dot_general x5 -> x0, matrix products: 19.1 us -> none  [the longest x1 10.3 us: body(): jnp.einsum('bp,bij->pij', hot, block_weight, precision=high, preferred_el...]
    all_gather x1 -> x0, blocking collectives: 8.83 us -> none  [body(): every = lax.all_gather(leaves, 'nodes', axis=0, tiled=True)]
    unnamed x6 -> x10, local copies, waits for them, and re-layouts: 0.61 us -> 6.48 us
    gather x3 -> x0, local copies, waits for them, and re-layouts: 3.37 us -> none  [the longest x1 2.2 us: body(): param_flow = jnp.where(own_live[:, None, None], own * outer[own_pair], 0.0)]
    transpose x1 -> x0, local copies, waits for them, and re-layouts: 2.95 us -> none  [body(): jnp.einsum('qcis,cjs->qcij', scaled, unit, precision=high, preferred_elem...]
    select_n x3 -> x0, other arithmetic: 2.51 us -> none  [the longest x2 2.42 us: body(): param_flow = jnp.where(own_live[:, None, None], own * outer[own_pair], 0.0)]
  transfers between devices with their start and end apart: 2 -> 0, of which waited for: 1 -> 0; matrix products, arithmetic and copies ran while one was open for 6% -> 0% of each run, Pallas kernels for 0% -> 0%
where the time goes in v2:
time: 103 us
  Pallas kernels  90.9 us (88%)
  local copies, waits for them, and re-layouts  9.15 us (9%)
  other arithmetic  1.55 us (2%)
  between operations  1.41 us (1%)
    pallas_call x1, Pallas kernels, fused(): pl.pallas_call(main_kernel, in_specs=[smem] * 4 + [vmem] * 6, out_specs=[...  88.3 us
    unnamed x10, local copies, waits for them, and re-layouts  6.48 us
    pallas_call x1, Pallas kernels, sum_weights(): pl.pallas_call(weight_kernel, grid_spec=pltpu.PrefetchScalarGridSpec(num_...  2.61 us

profile of v2, /device:TPU:0, one launch (start us, length us, event | category | flops | bytes accessed | tf_op | source)
XLA Modules:
  0.0 103.1 jit_solution(15502067588932984025)
XLA Ops:
  0.6 0.0 copy-start.1
  0.6 0.0 copy-start.2
  1.3 0.7 pad_add_fusion
  2.0 0.8 slice_bitcast_fusion.1
  2.8 0.7 fusion.1
  3.5 0.1 convert_reduce_fusion
  3.6 0.1 broadcast_in_dim.6
  3.7 0.1 convert_add_fusion
  3.7 0.1 add.21.select
  3.8 0.8 copy.13
  4.6 0.1 reshape.52.child_of
  4.7 0.1 broadcast_in_dim.14.mask
  4.8 0.1 copy.14
  4.9 0.1 reshape.53.pair_of
  5.0 1.3 %constant_dynamic-slice_fusion.own_weight = f32[16,128,128]{2,1,0:T(8,128)S(1)} fusion(f32[128,128,128]{2,1,0:T(8,128)} %w_ref.1, s32[]{:T(128)S(6)} %select_n.3), kind=kLoop, calls=%fused_computation.14 | loop fusion | bytes 2097156 | tf_op jit(solution)/shard_map/dynamic_slice | solution.py:392
  6.4 0.0 copy-start
  6.4 3.4 %copy-done = f32[128,128,128]{2,1,0:T(8,128)S(1)} copy-done((f32[128,128,128]{2,1,0:T(8,128)S(1)}, f32[128,128,128]{2,1,0:T(8,128)}, u32[]{:S(2)}) %copy-start) | copy-done | bytes 8388632
  9.7 2.6 %shard_map.94 = (bf16[32,128,128]{2,1,0:T(8,128)(2,1)S(1)}, bf16[32,128,128]{2,1,0:T(8,128)(2,1)S(1)}) custom-call(s32[128]{0:T(128)S(1)} %get-tuple-element.8.pair_ref, s32[1]{0:T(128)} %copy.18.count_ref, f32[128,128,128]{2,1,0:T(8,128)S(1)} %copy-done), custom_call_target="tpu_custom_call" | custom-call | tf_op jit(solution)/shard_map/pallas_call | solution.py:116
  12.4 0.0 copy-done.1
  12.4 0.0 copy-done.2
  12.4 88.3 %shard_map.95 = (f32[4,128,128]{2,1,0:T(8,128)S(1)}, f32[2,128,128]{2,1,0:T(8,128)S(1)}, f32[16,128,128]{2,1,0:T(8,128)S(1)}) custom-call(s32[16]{0:T(128)S(1)} %reshape.52.child_of, s32[256]{0:T(256)S(1)} %reshape.53.pair_of, f32[128]{0:T(128)S(1)} %get-tuple-element.12.alive, f32[64]{0:T(128)S(1)} %add.21.select, f32[2,128,128]{2,1,0:T(8,128)S(1)} %copy-done.2, ...), custom_call_target="tpu_custom_call" | custom-call | tf_op jit(solution)/shard_map/pallas_call | solution.py:397
  100.7 0.7 copy.19
  101.4 0.7 copy.20
  102.1 1.0 copy.21
  (1 shorter events, 0.0 us)
Async XLA Ops:
  0.6 11.7 %copy-start.1 = (f32[4,128,128]{2,1,0:T(8,128)S(1)}, f32[4,128,128]{2,1,0:T(8,128)}, u32[]{:S(2)}) copy-start(f32[4,128,128]{2,1,0:T(8,128)} %upper.1) | copy-start | bytes 786436
  0.6 11.7 %copy-start.2 = (f32[2,128,128]{2,1,0:T(8,128)S(1)}, f32[2,128,128]{2,1,0:T(8,128)}, u32[]{:S(2)}) copy-start(f32[2,128,128]{2,1,0:T(8,128)} %leaves.1) | copy-start | bytes 393220
  6.4 3.4 %copy-start = (f32[128,128,128]{2,1,0:T(8,128)S(1)}, f32[128,128,128]{2,1,0:T(8,128)}, u32[]{:S(2)}) copy-start(f32[128,128,128]{2,1,0:T(8,128)} %w_ref.1) | copy-start | bytes 25165828

commit v3 on v2

--- a/solution.py
+++ b/solution.py
@@ -85,17 +85,21 @@
     return dot(a_hi, b_hi) + dot(a_hi, b_lo) + dot(a_lo, b_hi)
 
 
-def weight_kernel(pair_ref, count_ref, w_ref, hi_ref, lo_ref, acc):
+def weight_kernel(child_ref, parent_ref, count_ref, w_ref, hi_ref, lo_ref, mask_ref, acc):
     step = pl.program_id(0)
     size = w_ref.shape[0]
+    sums = hi_ref.shape[0] // mask_ref.shape[1]
 
     @pl.when(step == 0)
     def _():
         acc[...] = jnp.zeros_like(acc)
+        mask_ref[...] = jnp.zeros_like(mask_ref)
 
     def add(b, carry):
-        at = pair_ref[step * size + b]
+        c, q = child_ref[0, step * size + b], parent_ref[0, step * size + b]
+        at = c * sums + q
         acc[at] = acc[at] + w_ref[b]
+        mask_ref[q, c] = jnp.ones(mask_ref.shape[2:], f32)
         return carry
 
     lax.fori_loop(0, jnp.clip(count_ref[0] - step * size, 0, size), add, 0)
@@ -109,29 +113,34 @@
         lax.fori_loop(0, acc.shape[0], out, 0)
 
 
-def sum_weights(block_weight, pair, count, pairs):
+def sum_weights(block_weight, child, parent, count, sums, prods, samples):
     blocks, rows, columns = block_weight.shape
     size = 16
+    pairs = sums * prods
     whole = pl.BlockSpec((pairs, rows, columns), lambda i, *_: (0, 0, 0))
     return pl.pallas_call(
         weight_kernel,
         grid_spec=pltpu.PrefetchScalarGridSpec(
-            num_scalar_prefetch=2,
+            num_scalar_prefetch=3,
             grid=(blocks // size,),
             in_specs=[pl.BlockSpec((size, rows, columns), lambda i, *_: (i, 0, 0))],
-            out_specs=[whole, whole],
+            out_specs=[
+                whole, whole, pl.BlockSpec((sums, prods, 1, samples), lambda i, *_: (0, 0, 0, 0))
+            ],
             scratch_shapes=[pltpu.VMEM((pairs, rows, columns), f32)],
         ),
-        out_shape=[jax.ShapeDtypeStruct((pairs, rows, columns), bf16)] * 2,
-        compiler_params=pltpu.CompilerParams(vmem_limit_bytes=24 << 20),
-    )(pair, count, block_weight)
+        out_shape=[jax.ShapeDtypeStruct((pairs, rows, columns), bf16)] * 2
+        + [jax.ShapeDtypeStruct((sums, prods, 1, samples), f32)],
+        compiler_params=pltpu.CompilerParams(vmem_limit_bytes=56 << 20),
+    )(child, parent, count, block_weight)
 
 
 def main_kernel(
-    child_of, pair_of, alive, select, leaves, w_hi, w_lo, mask, upper, own_weight,
+    child_of, child, parent, count, leaves, w_hi, w_lo, mask, upper, weight,
     sum_values, leaf_flow, param_flow,
-    L, F, cur, fcur, u_hi, u_lo, peaks, scale, total, outer, part, got_core, mid, got_x,
-    recv_l, send_lx, send_lc, send_ly, send_lz, recv_f, send_fy, send_fz, send_core, recv_core, send_x, recv_x,
+    L, F, cur, fcur, u_hi, u_lo, peaks, scale, cur_1, u_hi_1, u_lo_1, peaks_1, scale_1,
+    total, outer, own_weight, part, got_core, mid, got_x,
+    recv_l, send_lx, send_lc, send_ly, send_lz, recv_f, send_fy, send_fz, send_core, recv_core, send_x, recv_x, own_sem,
 ):
     n, t = lax.axis_index("nodes"), lax.axis_index("batch")
     x, k, z, y = n // 2, n % 2, t // 2, t % 2
@@ -141,10 +150,12 @@
     by_z = ((n, t - 2), (n, t + 2))
     has_z = (z > 0, z < depth - 1)
     prods, sums = u_hi.shape[0], upper.shape[0]
-    wide = upper.shape[1]
+    wide, samples = upper.shape[1:]
     keep = outer.shape[0]
     very = f32(very_low)
 
+    own_copy = pltpu.make_async_copy(weight.at[pl.ds(t * keep, keep)], own_weight, own_sem)
+    own_copy.start()
     L[t * 4 + n] = leaves[...]
     barrier = pltpu.get_barrier_semaphore()
     for partner in (by_x, by_core, by_y):
@@ -196,80 +207,134 @@
         leaf_x(tt).start()
         leaf_c(n, 0, tt).start()
 
-    def gather(tt):
+    def from_x(tt):
         arrived_l(nx, tt)
         leaf_c(nx, 1, tt).start()
+
+    def from_core(tt):
         arrived_l(nc, tt)
         arrived_l(nxc, tt)
 
-    def units(tt):
-        cur[...] = L[pl.ds(tt * 4, 4)].reshape(cur.shape)
-
-        def one(c, carry):
-            prod = cur[child_of[2 * c]] + cur[child_of[2 * c + 1]]
-            peak = jnp.max(prod, axis=0, keepdims=True)
-            peaks[c] = peak
-            u_hi[c], u_lo[c] = split(jnp.exp(prod - peak))
+    def each_side(step, act):
+        for side, zz, exists in ((0, z - step, z - step >= 0), (1, z + step, z + step < depth)):
+            @pl.when(exists)
+            def _():
+                act(side, zz)
+
+    def leaf_hop(side, zz):
+        arrived_l(n, zz * 2 + y)
+        @pl.when(has_z[1 - side])
+        def _():
+            leaf_z(zz, 1 - side).start()
+        leaf_y(zz).start()
+        spread(zz * 2 + y)
+
+    def flow_hop(side, zz):
+        arrived_f(zz * 2 + y)
+        @pl.when(has_z[1 - side])
+        def _():
+            flow_z(zz, 1 - side).start()
+        flow_y(zz).start()
+
+    def leaf_turn(side, zz):
+        arrived_l(n, zz * 2 + 1 - y)
+        spread(zz * 2 + 1 - y)
+
+    def both_x(side, zz):
+        for yy in range(2):
+            from_x(zz * 2 + yy)
+
+    def units(cur, u_hi, u_lo, peaks, scale):
+        times = cur.shape[-1] // samples
+
+        def some(i, carry):
+            for c in (2 * i, 2 * i + 1):
+                prod = cur[child_of[c, 0]] + cur[child_of[c, 1]]
+                peak = jnp.max(prod, axis=0, keepdims=True)
+                peaks[c] = peak
+                u_hi[c], u_lo[c] = split(jnp.exp(prod - peak))
             return carry
 
-        lax.fori_loop(0, prods, one, 0)
+        lax.fori_loop(0, prods // 2, some, 0)
         tops = []
         for q in range(sums):
-            on = mask[q] > 0.0
+            on = jnp.concatenate([mask[q]] * times, axis=-1) > 0.0
             top = jnp.max(jnp.where(on, peaks[...], very), axis=0, keepdims=True)
             scale[q] = jnp.where(on, jnp.exp(jnp.where(on, peaks[...] - top, 0.0)), 0.0)
             tops.append(top[0])
         return tops
 
-    def outers(tt, first):
-        fcur[...] = F[tt]
-
-        def one(b, carry):
-            q, c = pair_of[2 * (t * keep + b)], pair_of[2 * (t * keep + b) + 1]
-            f = split(fcur[q] * scale[q, c])
-            value = dot3(f, (u_hi[c], u_lo[c]), ((1,), (1,)))
-            outer[b] = value if first else outer[b] + value
+    def outers(zz):
+        for yy in range(2):
+            columns = pl.ds(yy * samples, samples)
+            cur[:, :, columns] = L[pl.ds((zz * 2 + yy) * 4, 4)].reshape(cur_1.shape)
+            fcur[:, :, columns] = F[zz * 2 + yy]
+        units(cur, u_hi, u_lo, peaks, scale)
+
+        def some(i, carry):
+            for j in range(4):
+                b = 4 * i + j
+                q, c = parent[0, t * keep + b], child[0, t * keep + b]
+                outer[b] += dot3(split(fcur[q] * scale[q, c]), (u_hi[c], u_lo[c]), ((1,), (1,)))
             return carry
 
-        lax.fori_loop(0, keep, one, 0)
-
-    leaf_x(t).start()
-    leaf_c(n, 0, t).start()
+        lax.fori_loop(0, keep // 4, some, 0)
+
+    def at_hop(step):
+        def one(side, carry):
+            zz = z + step * (2 * side - 1)
+
+            @pl.when((zz >= 0) & (zz < depth))
+            def _():
+                from_core(zz * 2)
+                from_core(zz * 2 + 1)
+                arrived_f(zz * 2 + 1 - y)
+                outers(zz)
+            return carry
+
+        lax.fori_loop(0, 2, one, 0)
+
+    spread(t)
     for side in range(2):
         @pl.when(has_z[side])
         def _():
             leaf_z(z, side).start()
     leaf_y(z).start()
-    gather(t)
-    tops = units(t)
+    outer[...] = jnp.zeros_like(outer)
     total[...] = jnp.zeros_like(total)
-
-    def ahead(c, carry):
-        value = dot3((w_hi[c], w_lo[c]), (u_hi[c], u_lo[c]), ((1,), (0,)))
-        for q in range(sums):
-            rows = pl.ds(q * wide, wide)
-            total[rows] += value[q * wide : (q + 1) * wide] * scale[q, c]
+    part[...] = jnp.zeros_like(part)
+    from_x(t)
+    from_core(t)
+    cur_1[...] = L[pl.ds(t * 4, 4)].reshape(cur_1.shape)
+    tops = units(cur_1, u_hi_1, u_lo_1, peaks_1, scale_1)
+
+    def ahead(i, carry):
+        for c in (2 * i, 2 * i + 1):
+            value = dot3((w_hi[c], w_lo[c]), (u_hi_1[c], u_lo_1[c]), ((1,), (0,)))
+            for q in range(sums):
+                total[q * wide : (q + 1) * wide] += value[q * wide : (q + 1) * wide] * scale_1[q, c]
         return carry
 
-    lax.fori_loop(0, prods, ahead, 0)
+    lax.fori_loop(0, prods // 2, ahead, 0)
     for q in range(sums):
-        tot = total[pl.ds(q * wide, wide)]
-        sum_values[q] = tops[q] + jnp.log(tot)
-        F[t, q] = upper[q] / tot
+        F[t, q] = upper[q] / total[q * wide : (q + 1) * wide]
     for side in range(2):
         @pl.when(has_z[side])
         def _():
             flow_z(z, side).start()
     flow_y(z).start()
-
-    part[...] = jnp.zeros_like(part)
+    each_side(1, leaf_hop)
+    leaf_turn(0, z)
+    for q in range(sums):
+        sum_values[q] = tops[q] + jnp.log(total[q * wide : (q + 1) * wide])
 
     def behind(c, carry):
-        f = jnp.concatenate([F[t, q] * scale[q, c] for q in range(sums)], axis=0)
+        f = jnp.concatenate([F[t, q] * scale_1[q, c] for q in range(sums)], axis=0)
         value = dot3((w_hi[c], w_lo[c]), split(f), ((0,), (0,)))
-        value = value * (u_hi[c].astype(f32) + u_lo[c].astype(f32))
+        value = value * (u_hi_1[c].astype(f32) + u_lo_1[c].astype(f32))
         for g in range(part.shape[0]):
-            part[g] += value * select[c * part.shape[0] + g]
+            times = (child_of[c, 0] == g).astype(f32) + (child_of[c, 1] == g).astype(f32)
+            part[g] += value * times
         return carry
 
     lax.fori_loop(0, prods, behind, 0)
@@ -281,62 +346,38 @@
 
     for xx in range(2):
         core_copy(xx).start()
-
-    outers(t, True)
+    each_side(2, leaf_hop)
+    each_side(1, leaf_turn)
+    each_side(1, flow_hop)
+    from_x(z * 2 + 1 - y)
     for xx in range(2):
         core_copy(xx).wait_recv()
         mid[xx] = part[pl.ds(2 * (xx * 2 + k), 2)] + got_core[xx]
     x_copy = remote(mid.at[1 - x], got_x, send_x, recv_x, by_x)
     x_copy.start()
 
-    def other(zz):
-        tt = zz * 2 + 1 - y
-        arrived_l(n, tt)
-        spread(tt)
-        gather(tt)
-        arrived_f(tt)
-        units(tt)
-        outers(tt, False)
-
-    other(z)
-
-    def hop(step, carry):
-        places = (z - step, z + step)
-        exists = (z - step >= 0, z + step < depth)
-        for side in range(2):
-            zz = places[side]
-            @pl.when(exists[side])
-            def _():
-                tt = zz * 2 + y
-                arrived_l(n, tt)
-                spread(tt)
-                leaf_y(zz).start()
-                @pl.when(has_z[1 - side])
-                def _():
-                    leaf_z(zz, 1 - side).start()
-                arrived_f(tt)
-                flow_y(zz).start()
-                @pl.when(has_z[1 - side])
-                def _():
-                    flow_z(zz, 1 - side).start()
-        for side in range(2):
-            zz = places[side]
-            @pl.when(exists[side])
-            def _():
-                tt = zz * 2 + y
-                gather(tt)
-                units(tt)
-                outers(tt, False)
-                other(zz)
-        return carry
-
-    lax.fori_loop(1, depth, hop, 0)
+    from_core(z * 2 + 1 - y)
+    arrived_f(z * 2 + 1 - y)
+    outers(z)
+    each_side(3, leaf_hop)
+    each_side(2, leaf_turn)
+    each_side(1, both_x)
+    each_side(2, flow_hop)
+    each_side(3, leaf_turn)
+    each_side(2, both_x)
+    at_hop(1)
+    each_side(3, flow_hop)
+    each_side(3, both_x)
+    at_hop(2)
+    at_hop(3)
 
     x_copy.wait_recv()
     leaf_flow[...] = mid[x] + got_x[...]
+    own_copy.wait()
 
     def finish(b, carry):
-        param_flow[b] = own_weight[b] * outer[b] * alive[t * keep + b]
+        alive = (t * keep + b < count[0]).astype(f32)
+        param_flow[b] = own_weight[b] * outer[b] * alive
         return carry
 
     lax.fori_loop(0, keep, finish, 0)
@@ -372,52 +413,47 @@
 def fused(leaves, prod_child, block_weight, block_child, block_parent, block_count, upper_flow):
     group, wide, samples = leaves.shape
     prods, sums = prod_child.shape[0], upper_flow.shape[0]
-    blocks = block_weight.shape[0]
     owners, batches = lax.axis_size("nodes"), lax.axis_size("batch")
-    keep = blocks // batches
-    child, parent = block_child.reshape(-1), block_parent.reshape(-1)
-    live = jnp.arange(blocks, dtype=jnp.int32) < block_count[0]
-    w_hi, w_lo = sum_weights(block_weight, child * sums + parent, block_count, prods * sums)
+    keep = block_weight.shape[0] // batches
+    w_hi, w_lo, mask = sum_weights(
+        block_weight, block_child, block_parent, block_count, sums, prods, samples
+    )
     w_hi = w_hi.reshape(prods, sums * wide, wide)
     w_lo = w_lo.reshape(prods, sums * wide, wide)
-    hit = live[:, None] & (
-        (parent * prods + child)[:, None] == jnp.arange(sums * prods, dtype=jnp.int32)[None]
-    )
-    mask = jnp.max(hit.astype(f32), axis=0).reshape(sums, prods, 1, 1)
-    mask = jnp.broadcast_to(mask, (sums, prods, 1, samples))
-    select = (
-        jax.nn.one_hot(prod_child[:, 0], owners * group, dtype=f32)
-        + jax.nn.one_hot(prod_child[:, 1], owners * group, dtype=f32)
-    ).reshape(-1)
-    own = lax.dynamic_slice_in_dim(block_weight, lax.axis_index("batch") * keep, keep, 0)
-    pair_of = jnp.stack([parent, child], axis=1).reshape(-1)
     smem, vmem = pl.BlockSpec(memory_space=pltpu.SMEM), pl.BlockSpec(memory_space=pltpu.VMEM)
     dma = lambda *dims: pltpu.SemaphoreType.DMA(dims)
-    tile = (wide, samples)
+    vec = lambda kind, *dims: pltpu.VMEM(dims, kind)
+    two = 2 * samples
     return pl.pallas_call(
         main_kernel,
-        in_specs=[smem] * 4 + [vmem] * 6,
+        in_specs=[smem] * 4 + [vmem] * 5 + [pl.BlockSpec(memory_space=pl.ANY)],
         out_specs=[vmem] * 3,
         out_shape=[
             jax.ShapeDtypeStruct(upper_flow.shape, f32),
             jax.ShapeDtypeStruct(leaves.shape, f32),
-            jax.ShapeDtypeStruct(own.shape, f32),
+            jax.ShapeDtypeStruct((keep, *block_weight.shape[1:]), f32),
         ],
         scratch_shapes=[
-            pltpu.VMEM((batches * owners, group, *tile), f32),
-            pltpu.VMEM((batches, sums, *tile), f32),
-            pltpu.VMEM((owners * group, *tile), f32),
-            pltpu.VMEM((sums, *tile), f32),
-            pltpu.VMEM((prods, *tile), bf16),
-            pltpu.VMEM((prods, *tile), bf16),
-            pltpu.VMEM((prods, 1, samples), f32),
-            pltpu.VMEM((sums, prods, 1, samples), f32),
-            pltpu.VMEM((sums * wide, samples), f32),
-            pltpu.VMEM(own.shape, f32),
-            pltpu.VMEM((owners * group, *tile), f32),
-            pltpu.VMEM((2, group, *tile), f32),
-            pltpu.VMEM((2, group, *tile), f32),
-            pltpu.VMEM((group, *tile), f32),
+            vec(f32, batches * owners, group, wide, samples),
+            vec(f32, batches, sums, wide, samples),
+            vec(f32, owners * group, wide, two),
+            vec(f32, sums, wide, two),
+            vec(bf16, prods, wide, two),
+            vec(bf16, prods, wide, two),
+            vec(f32, prods, 1, two),
+            vec(f32, sums, prods, 1, two),
+            vec(f32, owners * group, wide, samples),
+            vec(bf16, prods, wide, samples),
+            vec(bf16, prods, wide, samples),
+            vec(f32, prods, 1, samples),
+            vec(f32, sums, prods, 1, samples),
+            vec(f32, sums * wide, samples),
+            vec(f32, keep, *block_weight.shape[1:]),
+            vec(f32, keep, *block_weight.shape[1:]),
+            vec(f32, owners * group, wide, samples),
+            vec(f32, 2, group, wide, samples),
+            vec(f32, 2, group, wide, samples),
+            vec(f32, group, wide, samples),
             dma(batches * owners),
             dma(batches),
             dma(2 * batches),
@@ -430,13 +466,14 @@
             dma(2),
             pltpu.SemaphoreType.DMA,
             pltpu.SemaphoreType.DMA,
+            pltpu.SemaphoreType.DMA,
         ],
         compiler_params=pltpu.CompilerParams(
-            collective_id=0, has_side_effects=True, vmem_limit_bytes=32 << 20
+            collective_id=0, has_side_effects=True, vmem_limit_bytes=56 << 20
         ),
     )(
-        prod_child.reshape(-1), pair_of, live.astype(f32), select,
-        leaves, w_hi, w_lo, mask, upper_flow, own,
+        prod_child, block_child, block_parent, block_count,
+        leaves, w_hi, w_lo, mask, upper_flow, block_weight,
     )
 
 

time: 103 us -> 70.2 us (0.68)
  Pallas kernels: 90.9 us -> 61.7 us
  local copies, waits for them, and re-layouts: 9.15 us -> 6.88 us
  other arithmetic: 1.55 us -> 0 us
    pallas_call x1, Pallas kernels: 88.3 us -> 53.5 us  [fused(): pl.pallas_call(main_kernel, in_specs=[smem] * 4 + [vmem] * 5 + [pl.BlockS...]
    pallas_call x1, Pallas kernels: 2.61 us -> 8.19 us  [sum_weights(): pl.pallas_call(weight_kernel, grid_spec=pltpu.PrefetchScalarGridSpec(num_...]
    dynamic_slice x1 -> x0, local copies, waits for them, and re-layouts: 1.32 us -> none  [fused(): lax.dynamic_slice_in_dim(block_weight, lax.axis_index('batch') * keep, ke...]
    unnamed x10 -> x4, local copies, waits for them, and re-layouts: 6.48 us -> 6.88 us
where the time goes in v3:
time: 70.2 us; the launch traced here: 69.9 us
  Pallas kernels  61.7 us (88%)
  local copies, waits for them, and re-layouts  6.88 us (10%)
  between operations  1.29 us (2%)
    pallas_call x1, Pallas kernels, fused(): pl.pallas_call(main_kernel, in_specs=[smem] * 4 + [vmem] * 5 + [pl.BlockS...  53.5 us
    pallas_call x1, Pallas kernels, sum_weights(): pl.pallas_call(weight_kernel, grid_spec=pltpu.PrefetchScalarGridSpec(num_...  8.19 us
    unnamed x4, local copies, waits for them, and re-layouts  6.88 us

profile of v3, /device:TPU:0, one launch (start us, length us, event | category | flops | bytes accessed | tf_op | source)
XLA Modules:
  0.0 69.9 jit_solution(292779628392558467)
XLA Ops:
  1.3 1.3 %copy.10.child_of = s32[8,2]{1,0:T(8,128)} copy(s32[8,2]{0,1:T(2,128)} %param.8) | data formatting | bytes 128 | tf_op args[1]
  2.6 8.2 %shard_map.94 = (bf16[32,128,128]{2,1,0:T(8,128)(2,1)}, bf16[32,128,128]{2,1,0:T(8,128)(2,1)}, f32[4,8,1,128]{3,2,1,0:T(1,128)}) custom-call(s32[1,128]{1,0:T(1,128)} %child.1, s32[1,128]{1,0:T(1,128)} %parent.1, s32[1]{0:T(128)S(6)} %copy.14.count_ref.count, f32[128,128,128]{2,1,0:T(8,128)} %weight.1), custom_call_target="tpu_custom_call" | custom-call | tf_op jit(solution)/shard_map/pallas_call | solution.py:121
  10.8 53.5 %shard_map.95 = (f32[4,128,128]{2,1,0:T(8,128)}, f32[2,128,128]{2,1,0:T(8,128)}, f32[16,128,128]{2,1,0:T(8,128)}) custom-call(s32[8,2]{1,0:T(8,128)} %copy.10.child_of, s32[1,128]{1,0:T(1,128)} %child.1, s32[1,128]{1,0:T(1,128)} %parent.1, s32[1]{0:T(128)S(6)} %copy.14.count_ref.count, f32[2,128,128]{2,1,0:T(8,128)} %leaves.1, bf16[8,512,128]{2,1,0:T(8,128)(2,1)} %bitcast.2, ...), custom_call_target="tpu_custom_call" | custom-call | tf_op jit(solution)/shard_map/pallas_call | solution.py:427
  64.3 1.7 %copy.15 = f32[4,128,128]{2,1,0:T(8,128)} copy(f32[4,128,128]{2,1,0:T(8,128)} %get-tuple-element.12) | data formatting | bytes 524288
  66.0 1.6 %copy.16 = f32[2,128,128]{2,1,0:T(8,128)} copy(f32[2,128,128]{2,1,0:T(8,128)} %get-tuple-element.13) | data formatting | bytes 262144
  67.6 2.3 %copy.17 = f32[16,128,128]{2,1,0:T(8,128)} copy(f32[16,128,128]{2,1,0:T(8,128)} %get-tuple-element.14) | data formatting | bytes 2097152

commit v4 on v3

--- a/solution.py
+++ b/solution.py
@@ -1,3 +1,5 @@
+import functools
+
 import jax
 import jax.numpy as jnp
 from jax import lax
@@ -85,62 +87,52 @@
     return dot(a_hi, b_hi) + dot(a_hi, b_lo) + dot(a_lo, b_hi)
 
 
-def weight_kernel(child_ref, parent_ref, count_ref, w_ref, hi_ref, lo_ref, mask_ref, acc):
-    step = pl.program_id(0)
-    size = w_ref.shape[0]
-    sums = hi_ref.shape[0] // mask_ref.shape[1]
-
-    @pl.when(step == 0)
-    def _():
-        acc[...] = jnp.zeros_like(acc)
-        mask_ref[...] = jnp.zeros_like(mask_ref)
-
-    def add(b, carry):
-        c, q = child_ref[0, step * size + b], parent_ref[0, step * size + b]
-        at = c * sums + q
-        acc[at] = acc[at] + w_ref[b]
-        mask_ref[q, c] = jnp.ones(mask_ref.shape[2:], f32)
-        return carry
-
-    lax.fori_loop(0, jnp.clip(count_ref[0] - step * size, 0, size), add, 0)
-
-    @pl.when(step == pl.num_programs(0) - 1)
-    def _():
-        def out(p, carry):
-            hi_ref[p], lo_ref[p] = split(acc[p])
-            return carry
-
-        lax.fori_loop(0, acc.shape[0], out, 0)
-
-
-def sum_weights(block_weight, child, parent, count, sums, prods, samples):
-    blocks, rows, columns = block_weight.shape
-    size = 16
-    pairs = sums * prods
-    whole = pl.BlockSpec((pairs, rows, columns), lambda i, *_: (0, 0, 0))
+def order_kernel(sums, count_ref, child_ref, parent_ref, whole_ref, real_ref):
+    blocks = child_ref.shape[1]
+    shape = (blocks, blocks)
+    row = lax.broadcasted_iota(jnp.int32, shape, 0)
+    column = lax.broadcasted_iota(jnp.int32, shape, 1)
+    row_f, column_f = row.astype(f32), column.astype(f32)
+    lane = lax.broadcasted_iota(jnp.int32, (1, blocks), 1)
+    key = child_ref[...] * sums + parent_ref[...]
+    key = jnp.where(lane < count_ref[0], key, 1 << 20).astype(f32)
+    along = jnp.broadcast_to(key, shape)
+    down = along.T
+    before = (down < along) | ((down == along) & (row < column))
+    rank = jnp.sum(before.astype(f32), axis=0, keepdims=True)
+    rank_down = jnp.broadcast_to(rank, shape).T
+    total = lambda take, value: jnp.sum(jnp.where(take, value, 0.0), axis=0, keepdims=True)
+    here = rank_down == column_f
+    order = total(here, row_f)
+    same = total(here, down) == total(rank_down == column_f - 1.0, down)
+    keep = jnp.where(same & (lane > 0), 1.0, 0.0)
+    last = jnp.maximum(total(down <= column_f, jnp.ones(shape, f32)) - 1.0, 0.0)
+    used = jnp.minimum(total(down == column_f, jnp.ones(shape, f32)), 1.0)
+    whole_ref[0:1] = order.astype(jnp.int32)
+    whole_ref[1:2] = last.astype(jnp.int32)
+    real_ref[0:1] = keep
+    real_ref[1:2] = used
+
+
+def order_blocks(count, child, parent, sums):
+    smem, vmem = pl.BlockSpec(memory_space=pltpu.SMEM), pl.BlockSpec(memory_space=pltpu.VMEM)
     return pl.pallas_call(
-        weight_kernel,
-        grid_spec=pltpu.PrefetchScalarGridSpec(
-            num_scalar_prefetch=3,
-            grid=(blocks // size,),
-            in_specs=[pl.BlockSpec((size, rows, columns), lambda i, *_: (i, 0, 0))],
-            out_specs=[
-                whole, whole, pl.BlockSpec((sums, prods, 1, samples), lambda i, *_: (0, 0, 0, 0))
-            ],
-            scratch_shapes=[pltpu.VMEM((pairs, rows, columns), f32)],
-        ),
-        out_shape=[jax.ShapeDtypeStruct((pairs, rows, columns), bf16)] * 2
-        + [jax.ShapeDtypeStruct((sums, prods, 1, samples), f32)],
-        compiler_params=pltpu.CompilerParams(vmem_limit_bytes=56 << 20),
-    )(child, parent, count, block_weight)
+        functools.partial(order_kernel, sums),
+        in_specs=[smem, vmem, vmem],
+        out_specs=[vmem, vmem],
+        out_shape=[
+            jax.ShapeDtypeStruct((2, child.shape[1]), jnp.int32),
+            jax.ShapeDtypeStruct((2, child.shape[1]), f32),
+        ],
+    )(count, child, parent)
 
 
 def main_kernel(
-    child_of, child, parent, count, leaves, w_hi, w_lo, mask, upper, weight,
+    child_of, child, parent, count, whole, real, leaves, upper, weight,
     sum_values, leaf_flow, param_flow,
     L, F, cur, fcur, u_hi, u_lo, peaks, scale, cur_1, u_hi_1, u_lo_1, peaks_1, scale_1,
-    total, outer, own_weight, part, got_core, mid, got_x,
-    recv_l, send_lx, send_lc, send_ly, send_lz, recv_f, send_fy, send_fz, send_core, recv_core, send_x, recv_x, own_sem,
+    total, outer, W, runs, w_hi, w_lo, part, got_core, mid, got_x,
+    recv_l, send_lx, send_lc, send_ly, send_lz, recv_f, send_fy, send_fz, send_core, recv_core, send_x, recv_x, w_sem,
 ):
     n, t = lax.axis_index("nodes"), lax.axis_index("batch")
     x, k, z, y = n // 2, n % 2, t // 2, t % 2
@@ -154,8 +146,14 @@
     keep = outer.shape[0]
     very = f32(very_low)
 
-    own_copy = pltpu.make_async_copy(weight.at[pl.ds(t * keep, keep)], own_weight, own_sem)
-    own_copy.start()
+    blocks, pieces = W.shape[0], w_sem.shape[0]
+
+    def weight_copy(i):
+        at = pl.ds(i * (blocks // pieces), blocks // pieces)
+        return pltpu.make_async_copy(weight.at[at], W.at[at], w_sem.at[i])
+
+    for i in range(pieces):
+        weight_copy(i).start()
     L[t * 4 + n] = leaves[...]
     barrier = pltpu.get_barrier_semaphore()
     for partner in (by_x, by_core, by_y):
@@ -258,10 +256,13 @@
         lax.fori_loop(0, prods // 2, some, 0)
         tops = []
         for q in range(sums):
-            on = jnp.concatenate([mask[q]] * times, axis=-1) > 0.0
-            top = jnp.max(jnp.where(on, peaks[...], very), axis=0, keepdims=True)
-            scale[q] = jnp.where(on, jnp.exp(jnp.where(on, peaks[...] - top, 0.0)), 0.0)
-            tops.append(top[0])
+            used = [real[1, c * sums + q] for c in range(prods)]
+            top = peaks[0] + (used[0] - 1.0) * -very
+            for c in range(1, prods):
+                top = jnp.maximum(top, peaks[c] + (used[c] - 1.0) * -very)
+            for c in range(prods):
+                scale[q, c] = jnp.exp(jnp.minimum(peaks[c] - top, 0.0)) * used[c]
+            tops.append(top)
         return tops
 
     def outers(zz):
@@ -303,8 +304,30 @@
     outer[...] = jnp.zeros_like(outer)
     total[...] = jnp.zeros_like(total)
     part[...] = jnp.zeros_like(part)
+
+    for i in range(pieces):
+        weight_copy(i).wait()
+
+    def run(i, value):
+        for j in range(4):
+            at = 4 * i + j
+            value = value * real[0, at] + W[whole[0, at]]
+            runs[at] = value
+        return value
+
+    lax.fori_loop(0, blocks // 4, run, jnp.zeros(W.shape[1:], f32))
     from_x(t)
+
+    def pick(c, carry):
+        for q in range(sums):
+            p = c * sums + q
+            rows = pl.ds(q * wide, wide)
+            w_hi[c, rows], w_lo[c, rows] = split(runs[whole[1, p]] * real[1, p])
+        return carry
+
+    lax.fori_loop(0, prods, pick, 0)
     from_core(t)
+    each_side(1, leaf_hop)
     cur_1[...] = L[pl.ds(t * 4, 4)].reshape(cur_1.shape)
     tops = units(cur_1, u_hi_1, u_lo_1, peaks_1, scale_1)
 
@@ -323,8 +346,8 @@
         def _():
             flow_z(z, side).start()
     flow_y(z).start()
-    each_side(1, leaf_hop)
     leaf_turn(0, z)
+    each_side(2, leaf_hop)
     for q in range(sums):
         sum_values[q] = tops[q] + jnp.log(total[q * wide : (q + 1) * wide])
 
@@ -346,7 +369,6 @@
 
     for xx in range(2):
         core_copy(xx).start()
-    each_side(2, leaf_hop)
     each_side(1, leaf_turn)
     each_side(1, flow_hop)
     from_x(z * 2 + 1 - y)
@@ -373,11 +395,10 @@
 
     x_copy.wait_recv()
     leaf_flow[...] = mid[x] + got_x[...]
-    own_copy.wait()
 
     def finish(b, carry):
         alive = (t * keep + b < count[0]).astype(f32)
-        param_flow[b] = own_weight[b] * outer[b] * alive
+        param_flow[b] = W[t * keep + b] * outer[b] * alive
         return carry
 
     lax.fori_loop(0, keep, finish, 0)
@@ -415,18 +436,14 @@
     prods, sums = prod_child.shape[0], upper_flow.shape[0]
     owners, batches = lax.axis_size("nodes"), lax.axis_size("batch")
     keep = block_weight.shape[0] // batches
-    w_hi, w_lo, mask = sum_weights(
-        block_weight, block_child, block_parent, block_count, sums, prods, samples
-    )
-    w_hi = w_hi.reshape(prods, sums * wide, wide)
-    w_lo = w_lo.reshape(prods, sums * wide, wide)
+    whole, real = order_blocks(block_count, block_child, block_parent, sums)
     smem, vmem = pl.BlockSpec(memory_space=pltpu.SMEM), pl.BlockSpec(memory_space=pltpu.VMEM)
     dma = lambda *dims: pltpu.SemaphoreType.DMA(dims)
     vec = lambda kind, *dims: pltpu.VMEM(dims, kind)
     two = 2 * samples
     return pl.pallas_call(
         main_kernel,
-        in_specs=[smem] * 4 + [vmem] * 5 + [pl.BlockSpec(memory_space=pl.ANY)],
+        in_specs=[smem] * 6 + [vmem] * 2 + [pl.BlockSpec(memory_space=pl.ANY)],
         out_specs=[vmem] * 3,
         out_shape=[
             jax.ShapeDtypeStruct(upper_flow.shape, f32),
@@ -449,7 +466,10 @@
             vec(f32, sums, prods, 1, samples),
             vec(f32, sums * wide, samples),
             vec(f32, keep, *block_weight.shape[1:]),
-            vec(f32, keep, *block_weight.shape[1:]),
+            vec(f32, *block_weight.shape),
+            vec(f32, *block_weight.shape),
+            vec(bf16, prods, sums * wide, wide),
+            vec(bf16, prods, sums * wide, wide),
             vec(f32, owners * group, wide, samples),
             vec(f32, 2, group, wide, samples),
             vec(f32, 2, group, wide, samples),
@@ -466,14 +486,14 @@
             dma(2),
             pltpu.SemaphoreType.DMA,
             pltpu.SemaphoreType.DMA,
-            pltpu.SemaphoreType.DMA,
+            dma(8),
         ],
         compiler_params=pltpu.CompilerParams(
-            collective_id=0, has_side_effects=True, vmem_limit_bytes=56 << 20
+            collective_id=0, has_side_effects=True, vmem_limit_bytes=50 << 20
         ),
     )(
-        prod_child, block_child, block_parent, block_count,
-        leaves, w_hi, w_lo, mask, upper_flow, block_weight,
+        prod_child, block_child, block_parent, block_count, whole, real,
+        leaves, upper_flow, block_weight,
     )
 
 

time: 70.2 us -> 58.2 us (0.83)
  Pallas kernels: 61.7 us -> 49.1 us
  local copies, waits for them, and re-layouts: 6.88 us -> 7.6 us
    pallas_call x2, Pallas kernels: 61.7 us -> 49.1 us  [the longest x1 47.6 us: fused(): pl.pallas_call(main_kernel, in_specs=[smem] * 6 + [vmem] * 2 + [pl.BlockS...]
    unnamed x4 -> x16, local copies, waits for them, and re-layouts: 6.88 us -> 7.6 us
where the time goes in v4:
time: 58.2 us; the launch traced here: 58 us
  Pallas kernels  49.1 us (84%)
  local copies, waits for them, and re-layouts  7.6 us (13%)
  between operations  1.29 us (2%)
    pallas_call x1, Pallas kernels, fused(): pl.pallas_call(main_kernel, in_specs=[smem] * 6 + [vmem] * 2 + [pl.BlockS...  47.6 us
    unnamed x16, local copies, waits for them, and re-layouts  7.6 us
    pallas_call x1, Pallas kernels, order_blocks(): pl.pallas_call(functools.partial(order_kernel, sums), in_specs=[smem, vme...  1.46 us

profile of v4, /device:TPU:0, one launch (start us, length us, event | category | flops | bytes accessed | tf_op | source)
XLA Modules:
  0.0 58.0 jit_solution(8215279158776562947)
XLA Ops:
  1.3 1.5 %shard_map.94 = (s32[2,128]{1,0:T(2,128)}, f32[2,128]{1,0:T(2,128)}) custom-call(s32[1]{0:T(128)S(6)} %copy.14.count_ref.count, s32[1,128]{1,0:T(1,128)} %child.1, s32[1,128]{1,0:T(1,128)} %parent.1), custom_call_target="tpu_custom_call" | custom-call | tf_op jit(solution)/shard_map/pallas_call | solution.py:119
  2.7 0.8 %copy.10.child_of = s32[8,2]{1,0:T(8,128)S(1)} copy(s32[8,2]{0,1:T(2,128)} %param.8) | data formatting | bytes 128 | tf_op args[1]
  3.5 0.0 copy-start
  3.5 0.9 %copy-done = f32[4,128,128]{2,1,0:T(8,128)S(1)} copy-done((f32[4,128,128]{2,1,0:T(8,128)S(1)}, f32[4,128,128]{2,1,0:T(8,128)}, u32[]{:S(2)}) %copy-start) | copy-done | bytes 262168
  4.4 0.0 copy-start.1
  4.4 0.9 %copy-done.1 = f32[2,128,128]{2,1,0:T(8,128)S(1)} copy-done((f32[2,128,128]{2,1,0:T(8,128)S(1)}, f32[2,128,128]{2,1,0:T(8,128)}, u32[]{:S(2)}) %copy-start.1) | copy-done | bytes 131096
  5.3 0.0 copy-start.2
  5.4 0.7 %copy-done.2 = s32[2,128]{1,0:T(2,128)S(1)} copy-done((s32[2,128]{1,0:T(2,128)S(1)}, s32[2,128]{1,0:T(2,128)}, u32[]{:S(2)}) %copy-start.2) | copy-done | bytes 1048
  6.0 0.0 copy-start.3
  6.0 0.7 %copy-done.3 = f32[2,128]{1,0:T(2,128)S(1)} copy-done((f32[2,128]{1,0:T(2,128)S(1)}, f32[2,128]{1,0:T(2,128)}, u32[]{:S(2)}) %copy-start.3) | copy-done | bytes 1048
  6.7 0.0 copy-start.4
  6.7 0.7 %copy-done.4 = s32[1,128]{1,0:T(1,128)S(1)} copy-done((s32[1,128]{1,0:T(1,128)S(1)}, s32[1,128]{1,0:T(1,128)}, u32[]{:S(2)}) %copy-start.4) | copy-done | bytes 536
  7.4 0.0 copy-start.5
  7.4 0.7 %copy-done.5 = s32[1,128]{1,0:T(1,128)S(1)} copy-done((s32[1,128]{1,0:T(1,128)S(1)}, s32[1,128]{1,0:T(1,128)}, u32[]{:S(2)}) %copy-start.5) | copy-done | bytes 536
  8.0 47.6 %shard_map.95 = (f32[4,128,128]{2,1,0:T(8,128)S(1)}, f32[2,128,128]{2,1,0:T(8,128)S(1)}, f32[16,128,128]{2,1,0:T(8,128)S(1)}) custom-call(s32[8,2]{1,0:T(8,128)S(1)} %copy.10.child_of, s32[1,128]{1,0:T(1,128)S(1)} %copy-done.4, s32[1,128]{1,0:T(1,128)S(1)} %copy-done.5, s32[1]{0:T(128)S(6)} %copy.14.count_ref.count, s32[2,128]{1,0:T(2,128)S(1)} %copy-done.2, ...), custom_call_target="tpu_custom_call" | custom-call | tf_op jit(solution)/shard_map/pallas_call | solution.py:444
  55.7 0.7 %copy.15 = f32[4,128,128]{2,1,0:T(8,128)} copy(f32[4,128,128]{2,1,0:T(8,128)S(1)} %get-tuple-element.10) | data formatting | bytes 524288
  56.4 0.7 %copy.16 = f32[2,128,128]{2,1,0:T(8,128)} copy(f32[2,128,128]{2,1,0:T(8,128)S(1)} %get-tuple-element.11) | data formatting | bytes 262144
  57.0 1.0 %copy.17 = f32[16,128,128]{2,1,0:T(8,128)} copy(f32[16,128,128]{2,1,0:T(8,128)S(1)} %get-tuple-element.12) | data formatting | bytes 2097152
Async XLA Ops:
  3.5 0.9 %copy-start = (f32[4,128,128]{2,1,0:T(8,128)S(1)}, f32[4,128,128]{2,1,0:T(8,128)}, u32[]{:S(2)}) copy-start(f32[4,128,128]{2,1,0:T(8,128)} %upper.1) | copy-start | bytes 786436
  4.4 0.9 %copy-start.1 = (f32[2,128,128]{2,1,0:T(8,128)S(1)}, f32[2,128,128]{2,1,0:T(8,128)}, u32[]{:S(2)}) copy-start(f32[2,128,128]{2,1,0:T(8,128)} %leaves.1) | copy-start | bytes 393220
  5.3 0.7 %copy-start.2 = (s32[2,128]{1,0:T(2,128)S(1)}, s32[2,128]{1,0:T(2,128)}, u32[]{:S(2)}) copy-start(s32[2,128]{1,0:T(2,128)} %get-tuple-element.5.whole) | copy-start | bytes 3076
  6.0 0.7 %copy-start.3 = (f32[2,128]{1,0:T(2,128)S(1)}, f32[2,128]{1,0:T(2,128)}, u32[]{:S(2)}) copy-start(f32[2,128]{1,0:T(2,128)} %get-tuple-element.6.real) | copy-start | bytes 3076
  6.7 0.7 %copy-start.4 = (s32[1,128]{1,0:T(1,128)S(1)}, s32[1,128]{1,0:T(1,128)}, u32[]{:S(2)}) copy-start(s32[1,128]{1,0:T(1,128)} %child.1) | copy-start | bytes 1540
  7.4 0.7 %copy-start.5 = (s32[1,128]{1,0:T(1,128)S(1)}, s32[1,128]{1,0:T(1,128)}, u32[]{:S(2)}) copy-start(s32[1,128]{1,0:T(1,128)} %parent.1) | copy-start | bytes 1540

commit v5 on v4

--- a/solution.py
+++ b/solution.py
@@ -87,14 +87,14 @@
     return dot(a_hi, b_hi) + dot(a_hi, b_lo) + dot(a_lo, b_hi)
 
 
-def order_kernel(sums, count_ref, child_ref, parent_ref, whole_ref, real_ref):
-    blocks = child_ref.shape[1]
+def order_kernel(sums, count_ref, both_ref, whole_ref, real_ref):
+    blocks = both_ref.shape[1]
     shape = (blocks, blocks)
     row = lax.broadcasted_iota(jnp.int32, shape, 0)
     column = lax.broadcasted_iota(jnp.int32, shape, 1)
     row_f, column_f = row.astype(f32), column.astype(f32)
     lane = lax.broadcasted_iota(jnp.int32, (1, blocks), 1)
-    key = child_ref[...] * sums + parent_ref[...]
+    key = both_ref[0:1] * sums + both_ref[1:2]
     key = jnp.where(lane < count_ref[0], key, 1 << 20).astype(f32)
     along = jnp.broadcast_to(key, shape)
     down = along.T
@@ -112,27 +112,31 @@
     whole_ref[1:2] = last.astype(jnp.int32)
     real_ref[0:1] = keep
     real_ref[1:2] = used
+    whole_ref[2:4] = both_ref[...]
+    real_ref[2:3] = jnp.where(lane < count_ref[0], 1.0, 0.0)
 
 
 def order_blocks(count, child, parent, sums):
+    both = jnp.concatenate([child, parent], axis=0)
     smem, vmem = pl.BlockSpec(memory_space=pltpu.SMEM), pl.BlockSpec(memory_space=pltpu.VMEM)
     return pl.pallas_call(
         functools.partial(order_kernel, sums),
-        in_specs=[smem, vmem, vmem],
+        in_specs=[smem, vmem],
         out_specs=[vmem, vmem],
         out_shape=[
-            jax.ShapeDtypeStruct((2, child.shape[1]), jnp.int32),
-            jax.ShapeDtypeStruct((2, child.shape[1]), f32),
+            jax.ShapeDtypeStruct((4, child.shape[1]), jnp.int32),
+            jax.ShapeDtypeStruct((3, child.shape[1]), f32),
         ],
-    )(count, child, parent)
+        compiler_params=pltpu.CompilerParams(vmem_limit_bytes=50 << 20),
+    )(count, both)
 
 
 def main_kernel(
-    child_of, child, parent, count, whole, real, leaves, upper, weight,
+    child_of, whole, real, leaves, upper_in, weight,
     sum_values, leaf_flow, param_flow,
     L, F, cur, fcur, u_hi, u_lo, peaks, scale, cur_1, u_hi_1, u_lo_1, peaks_1, scale_1,
-    total, outer, W, runs, w_hi, w_lo, part, got_core, mid, got_x,
-    recv_l, send_lx, send_lc, send_ly, send_lz, recv_f, send_fy, send_fz, send_core, recv_core, send_x, recv_x, w_sem,
+    upper, total, outer, W, runs, w_hi, w_lo, part, got_core, mid, got_x,
+    recv_l, send_lx, send_lc, send_ly, send_lz, recv_f, send_fy, send_fz, send_core, recv_core, send_x, recv_x, send_lp, in_sem, w_sem,
 ):
     n, t = lax.axis_index("nodes"), lax.axis_index("batch")
     x, k, z, y = n // 2, n % 2, t // 2, t % 2
@@ -141,6 +145,7 @@
     by_x, by_core, by_y = (nx, t), (nc, t), (n, z * 2 + 1 - y)
     by_z = ((n, t - 2), (n, t + 2))
     has_z = (z > 0, z < depth - 1)
+    pair_z = z + 1 - 2 * (z % 2)
     prods, sums = u_hi.shape[0], upper.shape[0]
     wide, samples = upper.shape[1:]
     keep = outer.shape[0]
@@ -152,9 +157,12 @@
         at = pl.ds(i * (blocks // pieces), blocks // pieces)
         return pltpu.make_async_copy(weight.at[at], W.at[at], w_sem.at[i])
 
+    leaf_in = pltpu.make_async_copy(leaves, L.at[t * 4 + n], in_sem.at[0])
+    flow_in = pltpu.make_async_copy(upper_in, upper, in_sem.at[1])
+    leaf_in.start()
     for i in range(pieces):
         weight_copy(i).start()
-    L[t * 4 + n] = leaves[...]
+    flow_in.start()
     barrier = pltpu.get_barrier_semaphore()
     for partner in (by_x, by_core, by_y):
         pl.semaphore_signal(barrier, inc=1, device_id=partner, device_id_type=MESH)
@@ -162,6 +170,7 @@
         @pl.when(has_z[side])
         def _():
             pl.semaphore_signal(barrier, inc=1, device_id=by_z[side], device_id_type=MESH)
+    leaf_in.wait()
     pl.semaphore_wait(barrier, 3 + (z > 0).astype(jnp.int32) + (z < depth - 1).astype(jnp.int32))
 
     def remote(src, dst, send, recv, to):
@@ -224,7 +233,9 @@
         @pl.when(has_z[1 - side])
         def _():
             leaf_z(zz, 1 - side).start()
-        leaf_y(zz).start()
+        @pl.when(zz != pair_z)
+        def _():
+            leaf_y(zz).start()
         spread(zz * 2 + y)
 
     def flow_hop(side, zz):
@@ -238,6 +249,9 @@
         arrived_l(n, zz * 2 + 1 - y)
         spread(zz * 2 + 1 - y)
 
+    def leaf_pair():
+        return leaf_to(n, z * 2 + 1 - y, send_lp, (n, pair_z * 2 + y))
+
     def both_x(side, zz):
         for yy in range(2):
             from_x(zz * 2 + yy)
@@ -247,7 +261,7 @@
 
         def some(i, carry):
             for c in (2 * i, 2 * i + 1):
-                prod = cur[child_of[c, 0]] + cur[child_of[c, 1]]
+                prod = cur[child_of[0, c]] + cur[child_of[1, c]]
                 peak = jnp.max(prod, axis=0, keepdims=True)
                 peaks[c] = peak
                 u_hi[c], u_lo[c] = split(jnp.exp(prod - peak))
@@ -275,7 +289,7 @@
         def some(i, carry):
             for j in range(4):
                 b = 4 * i + j
-                q, c = parent[0, t * keep + b], child[0, t * keep + b]
+                q, c = whole[3, t * keep + b], whole[2, t * keep + b]
                 outer[b] += dot3(split(fcur[q] * scale[q, c]), (u_hi[c], u_lo[c]), ((1,), (1,)))
             return carry
 
@@ -317,6 +331,9 @@
 
     lax.fori_loop(0, blocks // 4, run, jnp.zeros(W.shape[1:], f32))
     from_x(t)
+    each_side(1, leaf_hop)
+    leaf_turn(0, z)
+    leaf_pair().start()
 
     def pick(c, carry):
         for q in range(sums):
@@ -327,9 +344,11 @@
 
     lax.fori_loop(0, prods, pick, 0)
     from_core(t)
-    each_side(1, leaf_hop)
     cur_1[...] = L[pl.ds(t * 4, 4)].reshape(cur_1.shape)
     tops = units(cur_1, u_hi_1, u_lo_1, peaks_1, scale_1)
+
+    each_side(2, leaf_hop)
+    flow_in.wait()
 
     def ahead(i, carry):
         for c in (2 * i, 2 * i + 1):
@@ -346,8 +365,7 @@
         def _():
             flow_z(z, side).start()
     flow_y(z).start()
-    leaf_turn(0, z)
-    each_side(2, leaf_hop)
+    each_side(3, leaf_hop)
     for q in range(sums):
         sum_values[q] = tops[q] + jnp.log(total[q * wide : (q + 1) * wide])
 
@@ -356,7 +374,7 @@
         value = dot3((w_hi[c], w_lo[c]), split(f), ((0,), (0,)))
         value = value * (u_hi_1[c].astype(f32) + u_lo_1[c].astype(f32))
         for g in range(part.shape[0]):
-            times = (child_of[c, 0] == g).astype(f32) + (child_of[c, 1] == g).astype(f32)
+            times = (child_of[0, c] == g).astype(f32) + (child_of[1, c] == g).astype(f32)
             part[g] += value * times
         return carry
 
@@ -381,7 +399,6 @@
     from_core(z * 2 + 1 - y)
     arrived_f(z * 2 + 1 - y)
     outers(z)
-    each_side(3, leaf_hop)
     each_side(2, leaf_turn)
     each_side(1, both_x)
     each_side(2, flow_hop)
@@ -397,8 +414,7 @@
     leaf_flow[...] = mid[x] + got_x[...]
 
     def finish(b, carry):
-        alive = (t * keep + b < count[0]).astype(f32)
-        param_flow[b] = W[t * keep + b] * outer[b] * alive
+        param_flow[b] = W[t * keep + b] * outer[b] * real[2, t * keep + b]
         return carry
 
     lax.fori_loop(0, keep, finish, 0)
@@ -406,6 +422,7 @@
     for xx in range(2):
         core_copy(xx).wait_send()
     x_copy.wait_send()
+    leaf_pair().wait_send()
 
     def sent(tt, carry):
         leaf_x(tt).wait_send()
@@ -416,7 +433,9 @@
     lax.fori_loop(0, 2 * depth, sent, 0)
 
     def sent_z(zz, carry):
-        leaf_y(zz).wait_send()
+        @pl.when(zz != pair_z)
+        def _():
+            leaf_y(zz).wait_send()
         flow_y(zz).wait_send()
         @pl.when((zz >= z) & has_z[0])
         def _():
@@ -443,7 +462,7 @@
     two = 2 * samples
     return pl.pallas_call(
         main_kernel,
-        in_specs=[smem] * 6 + [vmem] * 2 + [pl.BlockSpec(memory_space=pl.ANY)],
+        in_specs=[smem] * 3 + [pl.BlockSpec(memory_space=pl.ANY)] * 3,
         out_specs=[vmem] * 3,
         out_shape=[
             jax.ShapeDtypeStruct(upper_flow.shape, f32),
@@ -464,6 +483,7 @@
             vec(bf16, prods, wide, samples),
             vec(f32, prods, 1, samples),
             vec(f32, sums, prods, 1, samples),
+            vec(f32, sums, wide, samples),
             vec(f32, sums * wide, samples),
             vec(f32, keep, *block_weight.shape[1:]),
             vec(f32, *block_weight.shape),
@@ -486,14 +506,15 @@
             dma(2),
             pltpu.SemaphoreType.DMA,
             pltpu.SemaphoreType.DMA,
+            pltpu.SemaphoreType.DMA,
+            dma(2),
             dma(8),
         ],
         compiler_params=pltpu.CompilerParams(
             collective_id=0, has_side_effects=True, vmem_limit_bytes=50 << 20
         ),
     )(
-        prod_child, block_child, block_parent, block_count, whole, real,
-        leaves, upper_flow, block_weight,
+        prod_child.T, whole, real, leaves, upper_flow, block_weight,
     )
 
 

time: 58.2 us -> 54.7 us (0.940)
  local copies, waits for them, and re-layouts: 7.6 us -> 4.86 us
  Pallas kernels: 49.1 us -> 47.7 us
  other arithmetic: 0 us -> 0.68 us
    unnamed x16 -> x9, local copies, waits for them, and re-layouts: 7.6 us -> 4.86 us
    pallas_call x1, Pallas kernels: 1.46 us -> 0.22 us  [order_blocks(): pl.pallas_call(functools.partial(order_kernel, sums), in_specs=[smem, vme...]
    concatenate x0 -> x1, other arithmetic: none -> 0.68 us  [order_blocks(): both = jnp.concatenate([child, parent], axis=0)]
where the time goes in v5:
time: 54.7 us; the launch traced here: 54.5 us
  Pallas kernels  47.7 us (87%)
  local copies, waits for them, and re-layouts  4.86 us (9%)
  between operations  1.3 us (2%)
  other arithmetic  0.68 us (1%)
    pallas_call x1, Pallas kernels, fused(): pl.pallas_call(main_kernel, in_specs=[smem] * 3 + [pl.BlockSpec(memory_sp...  47.5 us
    unnamed x9, local copies, waits for them, and re-layouts  4.86 us

profile of v5, /device:TPU:0, one launch (start us, length us, event | category | flops | bytes accessed | tf_op | source)
XLA Modules:
  0.0 54.5 jit_solution(11530232984193703162)
XLA Ops:
  1.3 0.7 %pad_add_fusion.both_ref = s32[2,128]{1,0:T(2,128)S(1)} fusion(s32[1,128]{1,0:T(1,128)} %param.11, s32[1,128]{1,0:T(1,128)} %param.10), kind=kLoop, calls=%fused_computation | loop fusion | flops 256 | bytes 2048 | tf_op jit(solution)/shard_map/concatenate | solution.py:120
  2.0 0.2 shard_map.94
  2.2 0.0 copy-start
  2.2 0.9 %copy-done = f32[4,128,128]{2,1,0:T(8,128)S(1)} copy-done((f32[4,128,128]{2,1,0:T(8,128)S(1)}, f32[4,128,128]{2,1,0:T(8,128)}, u32[]{:S(2)}) %copy-start) | copy-done | bytes 262168
  3.1 0.0 copy-start.1
  3.1 0.9 %copy-done.1 = f32[2,128,128]{2,1,0:T(8,128)S(1)} copy-done((f32[2,128,128]{2,1,0:T(8,128)S(1)}, f32[2,128,128]{2,1,0:T(8,128)}, u32[]{:S(2)}) %copy-start.1) | copy-done | bytes 131096
  4.0 0.0 copy-start.2
  4.0 0.7 %copy-done.2 = s32[8,2]{0,1:T(2,128)S(1)} copy-done((s32[8,2]{0,1:T(2,128)S(1)}, s32[8,2]{0,1:T(2,128)}, u32[]{:S(2)}) %copy-start.2) | copy-done | bytes 88
  4.7 47.5 %shard_map.95 = (f32[4,128,128]{2,1,0:T(8,128)S(1)}, f32[2,128,128]{2,1,0:T(8,128)S(1)}, f32[16,128,128]{2,1,0:T(8,128)S(1)}) custom-call(s32[2,8]{1,0:T(2,128)S(1)} %bitcast.1, s32[4,128]{1,0:T(4,128)S(1)} %get-tuple-element.5.whole, f32[3,128]{1,0:T(4,128)S(1)} %get-tuple-element.6.real, f32[2,128,128]{2,1,0:T(8,128)S(1)} %copy-done.1, ...), custom_call_target="tpu_custom_call" | custom-call | tf_op jit(solution)/shard_map/pallas_call | solution.py:463
  52.2 0.7 %copy.14 = f32[4,128,128]{2,1,0:T(8,128)} copy(f32[4,128,128]{2,1,0:T(8,128)S(1)} %get-tuple-element.10) | data formatting | bytes 524288
  52.9 0.7 %copy.15 = f32[2,128,128]{2,1,0:T(8,128)} copy(f32[2,128,128]{2,1,0:T(8,128)S(1)} %get-tuple-element.11) | data formatting | bytes 262144
  53.5 1.0 %copy.16 = f32[16,128,128]{2,1,0:T(8,128)} copy(f32[16,128,128]{2,1,0:T(8,128)S(1)} %get-tuple-element.12) | data formatting | bytes 2097152
Async XLA Ops:
  2.2 1.0 %copy-start = (f32[4,128,128]{2,1,0:T(8,128)S(1)}, f32[4,128,128]{2,1,0:T(8,128)}, u32[]{:S(2)}) copy-start(f32[4,128,128]{2,1,0:T(8,128)} %upper_in.1) | copy-start | bytes 786436
  3.1 0.9 %copy-start.1 = (f32[2,128,128]{2,1,0:T(8,128)S(1)}, f32[2,128,128]{2,1,0:T(8,128)}, u32[]{:S(2)}) copy-start(f32[2,128,128]{2,1,0:T(8,128)} %leaves.1) | copy-start | bytes 393220
  4.0 0.7 %copy-start.2 = (s32[8,2]{0,1:T(2,128)S(1)}, s32[8,2]{0,1:T(2,128)}, u32[]{:S(2)}) copy-start(s32[8,2]{0,1:T(2,128)} %param.8) | copy-start | bytes 196

commit v6 on v5

--- a/solution.py
+++ b/solution.py
@@ -147,6 +147,7 @@
     has_z = (z > 0, z < depth - 1)
     pair_z = z + 1 - 2 * (z % 2)
     prods, sums = u_hi.shape[0], upper.shape[0]
+    each = sums // 2
     wide, samples = upper.shape[1:]
     keep = outer.shape[0]
     very = f32(very_low)
@@ -194,21 +195,21 @@
     def leaf_z(zz, side):
         return leaf_to(n, zz * 2 + y, send_lz.at[side * depth + zz], by_z[side])
 
-    def flow_to(tt, send, to):
-        at = F.at[tt]
-        return remote(at, at, send, recv_f.at[tt], to)
-
-    def flow_y(zz):
-        return flow_to(zz * 2 + y, send_fy.at[zz], by_y)
-
-    def flow_z(zz, side):
-        return flow_to(zz * 2 + y, send_fz.at[side * depth + zz], by_z[side])
+    def flow_to(tt, half, send, to):
+        at = F.at[tt * 2 + half]
+        return remote(at, at, send, recv_f.at[tt * 2 + half], to)
+
+    def flow_y(zz, half):
+        return flow_to(zz * 2 + y, half, send_fy.at[zz * 2 + half], by_y)
+
+    def flow_z(zz, side, half):
+        return flow_to(zz * 2 + y, half, send_fz.at[(side * depth + zz) * 2 + half], by_z[side])
 
     def arrived_l(nn, tt):
         leaf_to(nn, tt, send_lx.at[tt], by_x).wait_recv()
 
-    def arrived_f(tt):
-        flow_to(tt, send_fy.at[0], by_y).wait_recv()
+    def arrived_f(tt, half):
+        flow_to(tt, half, send_fy.at[0], by_y).wait_recv()
 
     def spread(tt):
         leaf_x(tt).start()
@@ -238,12 +239,16 @@
             leaf_y(zz).start()
         spread(zz * 2 + y)
 
-    def flow_hop(side, zz):
-        arrived_f(zz * 2 + y)
-        @pl.when(has_z[1 - side])
-        def _():
-            flow_z(zz, 1 - side).start()
-        flow_y(zz).start()
+    def flow_hop(step):
+        for half in range(2):
+            def act(side, zz):
+                arrived_f(zz * 2 + y, half)
+                @pl.when(has_z[1 - side])
+                def _():
+                    flow_z(zz, 1 - side, half).start()
+                flow_y(zz, half).start()
+
+            each_side(step, act)
 
     def leaf_turn(side, zz):
         arrived_l(n, zz * 2 + 1 - y)
@@ -283,7 +288,7 @@
         for yy in range(2):
             columns = pl.ds(yy * samples, samples)
             cur[:, :, columns] = L[pl.ds((zz * 2 + yy) * 4, 4)].reshape(cur_1.shape)
-            fcur[:, :, columns] = F[zz * 2 + yy]
+            fcur[:, :, columns] = F[pl.ds((zz * 2 + yy) * 2, 2)].reshape(upper.shape)
         units(cur, u_hi, u_lo, peaks, scale)
 
         def some(i, carry):
@@ -303,7 +308,8 @@
             def _():
                 from_core(zz * 2)
                 from_core(zz * 2 + 1)
-                arrived_f(zz * 2 + 1 - y)
+                for half in range(2):
+                    arrived_f(zz * 2 + 1 - y, half)
                 outers(zz)
             return carry
 
@@ -359,18 +365,19 @@
 
     lax.fori_loop(0, prods // 2, ahead, 0)
     for q in range(sums):
-        F[t, q] = upper[q] / total[q * wide : (q + 1) * wide]
-    for side in range(2):
-        @pl.when(has_z[side])
-        def _():
-            flow_z(z, side).start()
-    flow_y(z).start()
+        F[2 * t + q // each, q % each] = upper[q] / total[q * wide : (q + 1) * wide]
+    for half in range(2):
+        for side in range(2):
+            @pl.when(has_z[side])
+            def _():
+                flow_z(z, side, half).start()
+        flow_y(z, half).start()
     each_side(3, leaf_hop)
     for q in range(sums):
         sum_values[q] = tops[q] + jnp.log(total[q * wide : (q + 1) * wide])
 
     def behind(c, carry):
-        f = jnp.concatenate([F[t, q] * scale_1[q, c] for q in range(sums)], axis=0)
+        f = jnp.concatenate([F[2 * t + q // each, q % each] * scale_1[q, c] for q in range(sums)], axis=0)
         value = dot3((w_hi[c], w_lo[c]), split(f), ((0,), (0,)))
         value = value * (u_hi_1[c].astype(f32) + u_lo_1[c].astype(f32))
         for g in range(part.shape[0]):
@@ -388,7 +395,7 @@
     for xx in range(2):
         core_copy(xx).start()
     each_side(1, leaf_turn)
-    each_side(1, flow_hop)
+    flow_hop(1)
     from_x(z * 2 + 1 - y)
     for xx in range(2):
         core_copy(xx).wait_recv()
@@ -397,16 +404,17 @@
     x_copy.start()
 
     from_core(z * 2 + 1 - y)
-    arrived_f(z * 2 + 1 - y)
-    outers(z)
     each_side(2, leaf_turn)
     each_side(1, both_x)
-    each_side(2, flow_hop)
+    flow_hop(2)
+    for half in range(2):
+        arrived_f(z * 2 + 1 - y, half)
+    outers(z)
     each_side(3, leaf_turn)
     each_side(2, both_x)
+    flow_hop(3)
+    each_side(3, both_x)
     at_hop(1)
-    each_side(3, flow_hop)
-    each_side(3, both_x)
     at_hop(2)
     at_hop(3)
 
@@ -436,15 +444,18 @@
         @pl.when(zz != pair_z)
         def _():
             leaf_y(zz).wait_send()
-        flow_y(zz).wait_send()
+        for half in range(2):
+            flow_y(zz, half).wait_send()
         @pl.when((zz >= z) & has_z[0])
         def _():
             leaf_z(zz, 0).wait_send()
-            flow_z(zz, 0).wait_send()
+            for half in range(2):
+                flow_z(zz, 0, half).wait_send()
         @pl.when((zz <= z) & has_z[1])
         def _():
             leaf_z(zz, 1).wait_send()
-            flow_z(zz, 1).wait_send()
+            for half in range(2):
+                flow_z(zz, 1, half).wait_send()
         return carry
 
     lax.fori_loop(0, depth, sent_z, 0)
@@ -471,7 +482,7 @@
         ],
         scratch_shapes=[
             vec(f32, batches * owners, group, wide, samples),
-            vec(f32, batches, sums, wide, samples),
+            vec(f32, batches * 2, sums // 2, wide, samples),
             vec(f32, owners * group, wide, two),
             vec(f32, sums, wide, two),
             vec(bf16, prods, wide, two),
@@ -499,9 +510,9 @@
             dma(2 * batches),
             dma(batches // 2),
             dma(batches),
+            dma(2 * batches),
             dma(batches),
-            dma(batches // 2),
-            dma(batches),
+            dma(2 * batches),
             dma(2),
             dma(2),
             pltpu.SemaphoreType.DMA,

time: 54.7 us -> 53.2 us (0.973)
  Pallas kernels: 47.7 us -> 46.1 us
    pallas_call x1, Pallas kernels: 47.5 us -> 45.9 us  [fused(): pl.pallas_call(main_kernel, in_specs=[smem] * 3 + [pl.BlockSpec(memory_sp...]
where the time goes in v6:
time: 53.2 us; the launch traced here: 53 us
  Pallas kernels  46.1 us (87%)
  local copies, waits for them, and re-layouts  4.86 us (9%)
  between operations  1.3 us (2%)
  other arithmetic  0.68 us (1%)
    pallas_call x1, Pallas kernels, fused(): pl.pallas_call(main_kernel, in_specs=[smem] * 3 + [pl.BlockSpec(memory_sp...  45.9 us
    unnamed x9, local copies, waits for them, and re-layouts  4.86 us

profile of v6, /device:TPU:0, one launch (start us, length us, event | category | flops | bytes accessed | tf_op | source)
XLA Modules:
  0.0 53.0 jit_solution(6382089137846872817)
XLA Ops:
  1.3 0.7 %pad_add_fusion.both_ref = s32[2,128]{1,0:T(2,128)S(1)} fusion(s32[1,128]{1,0:T(1,128)} %param.11, s32[1,128]{1,0:T(1,128)} %param.10), kind=kLoop, calls=%fused_computation | loop fusion | flops 256 | bytes 2048 | tf_op jit(solution)/shard_map/concatenate | solution.py:120
  2.0 0.2 shard_map.94
  2.2 0.0 copy-start
  2.2 0.9 %copy-done = f32[4,128,128]{2,1,0:T(8,128)S(1)} copy-done((f32[4,128,128]{2,1,0:T(8,128)S(1)}, f32[4,128,128]{2,1,0:T(8,128)}, u32[]{:S(2)}) %copy-start) | copy-done | bytes 262168
  3.1 0.0 copy-start.1
  3.1 0.9 %copy-done.1 = f32[2,128,128]{2,1,0:T(8,128)S(1)} copy-done((f32[2,128,128]{2,1,0:T(8,128)S(1)}, f32[2,128,128]{2,1,0:T(8,128)}, u32[]{:S(2)}) %copy-start.1) | copy-done | bytes 131096
  4.0 0.0 copy-start.2
  4.0 0.7 %copy-done.2 = s32[8,2]{0,1:T(2,128)S(1)} copy-done((s32[8,2]{0,1:T(2,128)S(1)}, s32[8,2]{0,1:T(2,128)}, u32[]{:S(2)}) %copy-start.2) | copy-done | bytes 88
  4.7 45.9 %shard_map.95 = (f32[4,128,128]{2,1,0:T(8,128)S(1)}, f32[2,128,128]{2,1,0:T(8,128)S(1)}, f32[16,128,128]{2,1,0:T(8,128)S(1)}) custom-call(s32[2,8]{1,0:T(2,128)S(1)} %bitcast.1, s32[4,128]{1,0:T(4,128)S(1)} %get-tuple-element.5.whole, f32[3,128]{1,0:T(4,128)S(1)} %get-tuple-element.6.real, f32[2,128,128]{2,1,0:T(8,128)S(1)} %copy-done.1, ...), custom_call_target="tpu_custom_call" | custom-call | tf_op jit(solution)/shard_map/pallas_call | solution.py:474
  50.6 0.7 %copy.14 = f32[4,128,128]{2,1,0:T(8,128)} copy(f32[4,128,128]{2,1,0:T(8,128)S(1)} %get-tuple-element.10) | data formatting | bytes 524288
  51.3 0.7 %copy.15 = f32[2,128,128]{2,1,0:T(8,128)} copy(f32[2,128,128]{2,1,0:T(8,128)S(1)} %get-tuple-element.11) | data formatting | bytes 262144
  52.0 1.0 %copy.16 = f32[16,128,128]{2,1,0:T(8,128)} copy(f32[16,128,128]{2,1,0:T(8,128)S(1)} %get-tuple-element.12) | data formatting | bytes 2097152
Async XLA Ops:
  2.2 1.0 %copy-start = (f32[4,128,128]{2,1,0:T(8,128)S(1)}, f32[4,128,128]{2,1,0:T(8,128)}, u32[]{:S(2)}) copy-start(f32[4,128,128]{2,1,0:T(8,128)} %upper_in.1) | copy-start | bytes 786436
  3.1 0.9 %copy-start.1 = (f32[2,128,128]{2,1,0:T(8,128)S(1)}, f32[2,128,128]{2,1,0:T(8,128)}, u32[]{:S(2)}) copy-start(f32[2,128,128]{2,1,0:T(8,128)} %leaves.1) | copy-start | bytes 393220
  4.0 0.7 %copy-start.2 = (s32[8,2]{0,1:T(2,128)S(1)}, s32[8,2]{0,1:T(2,128)}, u32[]{:S(2)}) copy-start(s32[8,2]{0,1:T(2,128)} %param.8) | copy-start | bytes 196

commit v7 on v6

--- a/solution.py
+++ b/solution.py
@@ -146,6 +146,7 @@
     by_z = ((n, t - 2), (n, t + 2))
     has_z = (z > 0, z < depth - 1)
     pair_z = z + 1 - 2 * (z % 2)
+    at_end = (z == 0) | (z == depth - 1)
     prods, sums = u_hi.shape[0], upper.shape[0]
     each = sums // 2
     wide, samples = upper.shape[1:]
@@ -234,7 +235,7 @@
         @pl.when(has_z[1 - side])
         def _():
             leaf_z(zz, 1 - side).start()
-        @pl.when(zz != pair_z)
+        @pl.when((zz != pair_z) | at_end)
         def _():
             leaf_y(zz).start()
         spread(zz * 2 + y)
@@ -339,7 +340,9 @@
     from_x(t)
     each_side(1, leaf_hop)
     leaf_turn(0, z)
-    leaf_pair().start()
+    @pl.when(at_end)
+    def _():
+        leaf_pair().start()
 
     def pick(c, carry):
         for q in range(sums):
@@ -430,7 +433,9 @@
     for xx in range(2):
         core_copy(xx).wait_send()
     x_copy.wait_send()
-    leaf_pair().wait_send()
+    @pl.when(at_end)
+    def _():
+        leaf_pair().wait_send()
 
     def sent(tt, carry):
         leaf_x(tt).wait_send()
@@ -441,7 +446,7 @@
     lax.fori_loop(0, 2 * depth, sent, 0)
 
     def sent_z(zz, carry):
-        @pl.when(zz != pair_z)
+        @pl.when((zz != pair_z) | at_end)
         def _():
             leaf_y(zz).wait_send()
         for half in range(2):

time: 53.2 us -> 53 us (level)
  no operation moved by 1% of the time
where the time goes in v7:
time: 53 us; the launch traced here: 52.8 us
  Pallas kernels  46 us (87%)
  local copies, waits for them, and re-layouts  4.86 us (9%)
  between operations  1.3 us (2%)
  other arithmetic  0.68 us (1%)
    pallas_call x1, Pallas kernels, fused(): pl.pallas_call(main_kernel, in_specs=[smem] * 3 + [pl.BlockSpec(memory_sp...  45.8 us
    unnamed x9, local copies, waits for them, and re-layouts  4.86 us

profile of v7, /device:TPU:0, one launch (start us, length us, event | category | flops | bytes accessed | tf_op | source)
XLA Modules:
  0.0 52.8 jit_solution(2481939367643398793)
XLA Ops:
  1.3 0.7 %pad_add_fusion.both_ref = s32[2,128]{1,0:T(2,128)S(1)} fusion(s32[1,128]{1,0:T(1,128)} %param.11, s32[1,128]{1,0:T(1,128)} %param.10), kind=kLoop, calls=%fused_computation | loop fusion | flops 256 | bytes 2048 | tf_op jit(solution)/shard_map/concatenate | solution.py:120
  2.0 0.2 shard_map.94
  2.2 0.0 copy-start
  2.2 0.9 %copy-done = f32[4,128,128]{2,1,0:T(8,128)S(1)} copy-done((f32[4,128,128]{2,1,0:T(8,128)S(1)}, f32[4,128,128]{2,1,0:T(8,128)}, u32[]{:S(2)}) %copy-start) | copy-done | bytes 262168
  3.1 0.0 copy-start.1
  3.1 0.9 %copy-done.1 = f32[2,128,128]{2,1,0:T(8,128)S(1)} copy-done((f32[2,128,128]{2,1,0:T(8,128)S(1)}, f32[2,128,128]{2,1,0:T(8,128)}, u32[]{:S(2)}) %copy-start.1) | copy-done | bytes 131096
  4.0 0.0 copy-start.2
  4.0 0.7 %copy-done.2 = s32[8,2]{0,1:T(2,128)S(1)} copy-done((s32[8,2]{0,1:T(2,128)S(1)}, s32[8,2]{0,1:T(2,128)}, u32[]{:S(2)}) %copy-start.2) | copy-done | bytes 88
  4.7 45.8 %shard_map.95 = (f32[4,128,128]{2,1,0:T(8,128)S(1)}, f32[2,128,128]{2,1,0:T(8,128)S(1)}, f32[16,128,128]{2,1,0:T(8,128)S(1)}) custom-call(s32[2,8]{1,0:T(2,128)S(1)} %bitcast.1, s32[4,128]{1,0:T(4,128)S(1)} %get-tuple-element.5.whole, f32[3,128]{1,0:T(4,128)S(1)} %get-tuple-element.6.real, f32[2,128,128]{2,1,0:T(8,128)S(1)} %copy-done.1, ...), custom_call_target="tpu_custom_call" | custom-call | tf_op jit(solution)/shard_map/pallas_call | solution.py:479
  50.5 0.7 %copy.14 = f32[4,128,128]{2,1,0:T(8,128)} copy(f32[4,128,128]{2,1,0:T(8,128)S(1)} %get-tuple-element.10) | data formatting | bytes 524288
  51.2 0.7 %copy.15 = f32[2,128,128]{2,1,0:T(8,128)} copy(f32[2,128,128]{2,1,0:T(8,128)S(1)} %get-tuple-element.11) | data formatting | bytes 262144
  51.8 1.0 %copy.16 = f32[16,128,128]{2,1,0:T(8,128)} copy(f32[16,128,128]{2,1,0:T(8,128)S(1)} %get-tuple-element.12) | data formatting | bytes 2097152
Async XLA Ops:
  2.2 1.0 %copy-start = (f32[4,128,128]{2,1,0:T(8,128)S(1)}, f32[4,128,128]{2,1,0:T(8,128)}, u32[]{:S(2)}) copy-start(f32[4,128,128]{2,1,0:T(8,128)} %upper_in.1) | copy-start | bytes 786436
  3.1 0.9 %copy-start.1 = (f32[2,128,128]{2,1,0:T(8,128)S(1)}, f32[2,128,128]{2,1,0:T(8,128)}, u32[]{:S(2)}) copy-start(f32[2,128,128]{2,1,0:T(8,128)} %leaves.1) | copy-start | bytes 393220
  4.0 0.7 %copy-start.2 = (s32[8,2]{0,1:T(2,128)S(1)}, s32[8,2]{0,1:T(2,128)}, u32[]{:S(2)}) copy-start(s32[8,2]{0,1:T(2,128)} %param.8) | copy-start | bytes 196
